TPU v7x, 128 devices: a whole 4x4x4 slice. The times are simulated.
128 devices in a mesh: ctx: 8 (over x_hi, y), head: 8 (over z, core), var: 2 (over x_lo).
Axes of the slice: x: 4 (x_hi: 2, x_lo: 2; x = x_hi * 2 + x_lo), y: 4, z: 4, core: 2. Of those that a mesh axis runs over, the one named last changes fastest.
Arguments:
- sequence: bfloat16 [4096, 1536], P('ctx', 'head'), may hold values from -8 to 8
- deletions: int32 [8, 2], P('var'), parts along dimension 0, may hold values from 0 to 4096, as said below
- conv_taps: float32 [3, 1536], P(None, 'head'), may hold values from -3 to 3
- conv_bias: float32 [1536], P('head'), may hold values from -3 to 3
- w_proj: bfloat16 [1536, 3584], P(None, 'head'), may hold values from -1 to 1
- w_out: bfloat16 [1536, 1536], P('head'), may hold values from -0.15625 to 0.15625
- w_pair: bfloat16 [1536, 256], P('head'), may hold values from -0.15625 to 0.15625
- dist_table: float32 [16, 128], replicated, may hold values from -3 to 3
Outputs:
- pair_map: bfloat16 [8, 1024, 1024, 128], P('var', 'ctx', 'head'), parts along dimension 0
There are 2 independent parts, one for each index of `var`. A program takes and returns all parts, laid end to end along the dimension named above; an argument that names none is the same for every part. Nothing has to cross between parts.
Inputs may be any that keep to these rules, and one draw needn't show every extreme that they name: `deletions`: each variant deletes 1 to 128 consecutive tokens, some variant deletes exactly 128, and some variant's deletion ends at the last token of the locus.
All inputs are finite; a program needn't handle non-finite values.
Results may differ from a plain program's by a relative error of at most 0.025.
Values may be sent and summed in bfloat16 or wider, within the bound.
A program may use at most 128 MiB of HBM per device.

v0:
```python
import math

import jax
import jax.numpy as jnp
from jax import lax
from jax.sharding import PartitionSpec as P

HD = 128
VD = 192
C = 128
NB = 16
POOL = 4


def extended(block, sides, width):
    for axis, dim in sides:
        count = lax.axis_size(axis)
        forward = [(i, i + 1) for i in range(count - 1)]
        backward = [(target, source) for source, target in forward]
        low = lax.ppermute(
            lax.slice_in_dim(block, block.shape[dim] - width, None, axis=dim), axis, forward
        )
        high = lax.ppermute(lax.slice_in_dim(block, 0, width, axis=dim), axis, backward)
        block = jnp.concatenate([low, block, high], axis=dim)
    return block


def attend_block(running, queries, key_rows, value_rows):
    row_max, row_sum, weighted = running
    scores = jnp.einsum(
        "vqhe,vkhe->vhqk", queries, key_rows, preferred_element_type=jnp.float32
    ) / math.sqrt(queries.shape[-1])
    new_max = jnp.maximum(row_max, scores.max(-1))
    shrink = jnp.exp(row_max - new_max)
    weights = jnp.exp(scores - new_max[..., None])
    row_sum = row_sum * shrink + weights.sum(-1)
    weighted = weighted * shrink[..., None] + jnp.einsum(
        "vhqk,vkhe->vhqe",
        weights.astype(jnp.bfloat16),
        value_rows,
        preferred_element_type=jnp.float32,
    )
    return (new_max, row_sum, weighted)


def attend_rows(running, queries, key_rows, value_rows):
    key_total = key_rows.shape[1]
    block_rows = 512
    block_count = key_total // block_rows

    def block_step(block_index, state_now):
        key_part = lax.dynamic_slice_in_dim(key_rows, block_index * block_rows, block_rows, 1)
        value_part = lax.dynamic_slice_in_dim(value_rows, block_index * block_rows, block_rows, 1)
        return attend_block(state_now, queries, key_part, value_part)

    return lax.fori_loop(0, block_count, block_step, running)


def local(sequence, deletions, conv_taps, conv_bias, w_proj, w_out, w_pair, dist_table):
    token_count, local_width = sequence.shape
    variants = deletions.shape[0]
    head_count = w_out.shape[0] // VD
    row_start = lax.axis_index("ctx") * token_count
    positions = row_start + jnp.arange(token_count, dtype=jnp.int32)
    kept = jnp.logical_or(
        positions[None, :] < deletions[:, 0:1], positions[None, :] >= deletions[:, 1:2]
    )
    masked = jnp.where(kept[:, :, None], sequence[None], jnp.zeros((), jnp.bfloat16))
    dilation = token_count // 2
    padded = extended(masked, (("ctx", 1),), dilation)
    spread = padded.astype(jnp.float32)
    middle = spread[:, dilation : dilation + token_count]
    convolved = (
        conv_taps[0] * spread[:, :token_count]
        + conv_taps[1] * middle
        + conv_taps[2] * spread[:, 2 * dilation : 2 * dilation + token_count]
        + conv_bias
    )
    trunk_out = (middle + jax.nn.gelu(convolved, approximate=True)).astype(jnp.bfloat16)
    projected = jnp.einsum(
        "vtd,df->vtf",
        lax.all_gather(trunk_out, "head", axis=2, tiled=True),
        w_proj,
        preferred_element_type=jnp.float32,
    ).astype(jnp.bfloat16)
    projected = projected.reshape(trunk_out.shape[0], token_count, head_count, 2 * HD + VD)
    queries = projected[:variants, :, :, :HD]
    key_rows = projected[:, :, :, HD : 2 * HD]
    value_rows = projected[:, :, :, 2 * HD :]
    running = attend_rows(
        (
            jnp.full((variants, head_count, token_count), -jnp.inf, jnp.float32),
            jnp.zeros((variants, head_count, token_count), jnp.float32),
            jnp.zeros((variants, head_count, token_count, VD), jnp.float32),
        ),
        queries,
        lax.all_gather(key_rows, "ctx", axis=1, tiled=True),
        lax.all_gather(value_rows, "ctx", axis=1, tiled=True),
    )
    row_max, row_sum, weighted = running
    head_out = (weighted / row_sum[..., None]).astype(jnp.bfloat16)
    flat_out = head_out.transpose(0, 2, 1, 3).reshape(variants * token_count, head_count * VD)
    mixed_back = lax.psum_scatter(
        lax.dot_general(
            w_out, flat_out, (((0,), (1,)), ((), ())), preferred_element_type=jnp.float32
        ).astype(jnp.bfloat16),
        "head",
        scatter_dimension=0,
        tiled=True,
    ).astype(jnp.float32)
    residual = trunk_out.astype(jnp.float32) + mixed_back.T.reshape(
        variants, token_count, local_width
    )
    pooled = (
        residual.reshape(variants, token_count // POOL, POOL, local_width)
        .mean(2)
        .astype(jnp.bfloat16)
    )
    partial_value = jnp.einsum("vpd,dc->vpc", pooled, w_pair, preferred_element_type=jnp.float32)
    pair_proj = lax.psum(partial_value.astype(jnp.bfloat16), "head").astype(jnp.float32)
    row_feats = pair_proj[:, :, :C]
    all_cols = lax.all_gather(
        pair_proj[:, :, C:].astype(jnp.bfloat16), "ctx", axis=1, tiled=True
    ).astype(jnp.float32)
    col_count = all_cols.shape[1] // lax.axis_size("head")
    col_start = lax.axis_index("head") * col_count
    col_feats = lax.dynamic_slice_in_dim(all_cols, col_start, col_count, 1)
    row_ids = lax.axis_index("ctx") * (token_count // POOL) + jnp.arange(
        token_count // POOL, dtype=jnp.int32
    )
    col_ids = col_start + jnp.arange(col_count, dtype=jnp.int32)
    distance = jnp.abs(row_ids[:, None] - col_ids[None, :])
    buckets = jnp.zeros(distance.shape, jnp.int32)
    for power_index in range(NB - 1):
        buckets = buckets + (distance >= 2**power_index).astype(jnp.int32)
    one_hot = (buckets[:, :, None] == jnp.arange(NB, dtype=jnp.int32)).astype(jnp.float32)
    rel_table = jnp.dot(one_hot, dist_table, precision=lax.Precision.HIGHEST)
    pair_map = row_feats[:, :, None, :] + col_feats[:, None, :, :] + rel_table[None]
    return pair_map.astype(jnp.bfloat16)


def solution(mesh):
    in_specs = (
        P("ctx", "head"),
        P("var", None),
        P(None, "head"),
        P("head"),
        P(None, "head"),
        P("head", None),
        P("head", None),
        P(),
    )
    out_specs = P("var", "ctx", "head", None)
    return jax.shard_map(local, mesh=mesh, in_specs=in_specs, out_specs=out_specs, check_vma=False)
```

profile of v0, /device:TPU:1, one launch (start us, length us, event | category | flops | bytes accessed | tf_op | source)
XLA Modules:
  0.0 485.4 jit_solution(6132765217847577570)
XLA Ops:
  8.5 4.1 collective-permute-start
  13.9 6.4 %collective-permute-done = bf16[4,256,192]{1,2,0:T(8,128)(2,1)S(1)} collective-permute-done((bf16[4,256,192]{1,2,0:T(8,128)(2,1)S(1)}, bf16[4,256,192]{1,2,0:T(8,128)(2,1)S(1)}, u32[]{:S(2)}, u32[]{:S(2)}) %collective-permute-start) | collective-permute-done | bytes 393248 | tf_op jit(solution)/shard_map/ppermute | solution.py:20
  20.3 3.8 collective-permute-done.1
  28.4 47.3 %all-gather.5.cloned.1.call-done = bf16[4,512,1536]{1,2,0:T(8,128)(2,1)} async-done(((bf16[4,512,192]{1,2,0:T(8,128)(2,1)}), bf16[4,512,1536]{1,2,0:T(8,128)(2,1)}) %all-gather.5.cloned.1.call-update) | async-done | bytes 6291472 | tf_op jit(solution)/shard_map/all_gather | solution.py:82
  75.7 5.8 %convert_bitcast_fusion = bf16[4,512,1,448]{1,3,0,2:T(8,128)(2,1)S(1)} fusion(bf16[4,512,1536]{1,2,0:T(8,128)(2,1)} %all-gather.5.cloned.1.call-done, bf16[1536,448]{0,1:T(8,128)(2,1)S(1)} %copy-done), kind=kOutput, calls=%fused_computation.29 | convolution fusion | flops 2819489792 | bytes 9502720 | tf_op jit(solution)/shard_map/vtd,df->vtf/dot_general | solution.py:80
  86.1 70.3 %all-gather.7.cloned.1.call-done = bf16[4,4096,1,128]{1,3,0,2:T(8,128)(2,1)} async-done(((bf16[4,512,1,128]{1,3,0,2:T(8,128)(2,1)}), bf16[4,4096,1,128]{1,3,0,2:T(8,128)(2,1)}) %all-gather.7.cloned.1.call-update) | async-done | bytes 4194320 | tf_op jit(solution)/shard_map/all_gather | solution.py:97
  156.4 93.5 %all-gather.9.cloned.1.call-done = bf16[4,4096,1,192]{1,3,0,2:T(8,128)(2,1)} async-done(((bf16[4,512,1,192]{1,3,0,2:T(8,128)(2,1)}), bf16[4,4096,1,192]{1,3,0,2:T(8,128)(2,1)}) %all-gather.9.cloned.1.call-update) | async-done | bytes 6291472 | tf_op jit(solution)/shard_map/all_gather | solution.py:98
  249.9 40.1 %while.18 = (s32[]{:T(128)}, f32[4,1,512]{2,0,1:T(4,128)S(1)}, f32[4,1,512]{2,0,1:T(4,128)S(1)}, f32[4,1,512,192]{2,3,0,1:T(8,128)S(1)}, bf16[4,4096,1,128]{1,3,...) while((s32[]{:T(128)}, f32[4,1,512]{2,0,1:T(4,128)S(1)}, ...), condition=%wide.region_3.4_spmd.clone, body=%wide.region_0.3_spmd.clone.sunk | while | flops 680669184 | bytes 17694904 | solution.py:56
  252.5 2.4 bitcast_add_fusion.5
  257.5 2.4 bitcast_add_fusion.5
  262.5 2.4 bitcast_add_fusion.5
  272.6 2.4 bitcast_add_fusion.5
  277.6 2.4 bitcast_add_fusion.5
  282.6 2.4 bitcast_add_fusion.5
  287.6 2.4 bitcast_add_fusion.5
  291.4 4.5 fusion.19
  295.9 8.7 %copy.38 = bf16[1536,2048]{1,0:T(8,128)(2,1)} copy(bf16[1536,2048]{0,1:T(8,128)(2,1)} %fusion.19) | data formatting | bytes 12582912
  304.9 40.2 %reduce-scatter.4.cloned.1.call-done = bf16[192,2048]{1,0:T(8,128)(2,1)} async-done(((bf16[1536,2048]{1,0:T(8,128)(2,1)}), bf16[192,2048]{1,0:T(8,128)(2,1)}) %reduce-scatter.4.cloned.1.call-update) | async-done | bytes 786448
  348.1 2.9 copy.32
  351.0 3.6 convert_add_fusion
  358.6 58.4 %all-reduce.2.cloned.1.call-done = bf16[4,128,256]{2,1,0:T(8,128)(2,1)} async-done(((bf16[4,128,256]{2,1,0:T(8,128)(2,1)}), bf16[4,128,256]{2,1,0:T(8,128)(2,1)}) %all-reduce.2.cloned.1.call-update) | async-done | bytes 262160 | tf_op jit(solution)/shard_map/psum | solution.py:120
  418.8 8.9 %fusion.33 = f32[128,128,128]{2,1,0:T(8,128)} fusion(s32[128,128]{1,0:T(8,128)S(1)} %convert_add_fusion.1, f32[16,128]{1,0:T(8,128)S(1)} %copy-done.7), kind=kOutput, calls=%fused_computation.50 | convolution fusion | flops 402915328 | bytes 8462336 | tf_op jit(solution)/shard_map/dot_general | solution.py:137
  427.7 37.5 %all-gather.11.cloned.1.call-done = bf16[4,1024,128]{2,1,0:T(8,128)(2,1)} async-done(((bf16[4,128,128]{2,1,0:T(8,128)(2,1)}), bf16[4,1024,128]{2,1,0:T(8,128)(2,1)}) %all-gather.11.cloned.1.call-update) | async-done | bytes 1048592 | tf_op jit(solution)/shard_map/all_gather | solution.py:122
  466.1 12.4 %add_convert_fusion = bf16[4,128,128,128]{3,2,1,0:T(8,128)(2,1)} fusion(f32[128,128,128]{2,1,0:T(8,128)} %fusion.33, f32[4,128,128]{2,1,0:T(8,128)S(1)} %dynamic-slice_convert_fusion, f32[4,128,128]{2,1,0:T(8,128)S(1)} %get-tuple-element.206), kind=kLoop, calls=%fused_computation.24 | loop fusion | flops 25165824 | bytes 25690112 | tf_op jit(solution)/shard_map/convert_element_type | solution.py:139
  (101 shorter events, 46.0 us)
Async XLA Ops:
  6.5 69.2 %copy-start = (bf16[1536,448]{0,1:T(8,128)(2,1)S(1)}, bf16[1536,448]{0,1:T(8,128)(2,1)}, u32[]{:S(2)}) copy-start(bf16[1536,448]{0,1:T(8,128)(2,1)} %param.14) | copy-start | bytes 4128772
  6.5 7.3 %copy-start.9 = (f32[3,192]{1,0:T(4,128)S(1)}, f32[3,192]{1,0:T(4,128)}, u32[]{:S(2)}) copy-start(f32[3,192]{1,0:T(4,128)} %param.12) | copy-start | bytes 6916
  6.5 69.1 %all-gather.5.cloned.1.call-start = ((), (), s32[]{:S(2)}) async-start(), calls=%async_computation.1 | async-start | bytes 7077888 | tf_op jit(solution)/shard_map/all_gather | solution.py:82
  8.5 11.8 %collective-permute-start = (bf16[4,256,192]{1,2,0:T(8,128)(2,1)S(1)}, bf16[4,256,192]{1,2,0:T(8,128)(2,1)S(1)}, u32[]{:S(2)}, u32[]{:S(2)}) collective-permute-start(bf16[4,256,192]{1,2,0:T(8,128)(2,1)S(1)} %get-tuple-element.204), channel_id=1, source_target_pairs={{0,16},{16,32},{32,48},{48,64},{64,80},{80,96},{96,112},{1,17},{17... | collective-permute-start | bytes 1179656 | tf_op jit(solution)/shard_map/ppermute | solution.py:20
  12.6 11.6 %collective-permute-start.1 = (bf16[4,256,192]{1,2,0:T(8,128)(2,1)S(1)}, bf16[4,256,192]{1,2,0:T(8,128)(2,1)S(1)}, u32[]{:S(2)}, u32[]{:S(2)}) collective-permute-start(bf16[4,256,192]{1,2,0:T(8,128)(2,1)S(1)} %get-tuple-element.205), channel_id=1, source_target_pairs={{16,0},{32,16},{48,32},{64,48},{80,64},{96,80},{112,96},{17,1},{33... | collective-permute-start | bytes 1179656 | tf_op jit(solution)/shard_map/ppermute | solution.py:23
  13.9 12.5 %copy-start.8 = (f32[192]{0:T(256)S(1)}, f32[192]{0:T(256)}, u32[]{:S(2)}) copy-start(f32[192]{0:T(256)} %param.13) | copy-start | bytes 2308
  24.5 1.8 copy-start.2
  28.3 128.1 %all-gather.7.cloned.1.call-start = ((), (), s32[]{:S(2)}) async-start(), calls=%async_computation.2 | async-start | bytes 4718592 | tf_op jit(solution)/shard_map/all_gather | solution.py:97
  81.5 1.2 copy-start.4
  83.6 166.3 %all-gather.9.cloned.1.call-start = ((), (), s32[]{:S(2)}) async-start(), calls=%async_computation.3 | async-start | bytes 7077888 | tf_op jit(solution)/shard_map/all_gather | solution.py:98
  85.8 259.4 %reduce-scatter.4.cloned.1.call-start = ((), (), s32[]{:S(2)}) async-start(), calls=%async_computation.6 | async-start | bytes 7077888
  290.3 1.1 copy-start.5
  304.7 112.3 %all-reduce.2.cloned.1.call-start = ((), (), s32[]{:S(2)}) async-start(), calls=%async_computation.4 | async-start | bytes 524288 | tf_op jit(solution)/shard_map/psum | solution.py:120
  348.1 2.9 copy-start.3
  356.6 0.9 copy-start.6
  357.2 61.6 %copy-start.7 = (f32[16,128]{1,0:T(8,128)S(1)}, f32[16,128]{1,0:T(8,128)}, u32[]{:S(2)}) copy-start(f32[16,128]{1,0:T(8,128)} %param.17) | copy-start | bytes 24580
  358.5 106.7 %all-gather.11.cloned.1.call-start = ((), (), s32[]{:S(2)}) async-start(), calls=%async_computation.5 | async-start | bytes 1179648 | tf_op jit(solution)/shard_map/all_gather | solution.py:122
  466.1 12.4 %copy-start.1 = (bf16[1536,448]{0,1:T(8,128)(2,1)S(1)}, bf16[1536,448]{0,1:T(8,128)(2,1)}, u32[]{:S(2)}) copy-start(bf16[1536,448]{0,1:T(8,128)(2,1)} %param.14) | copy-start | bytes 4128772
Sparse Core Ops, SparseCore 0:
  28.4 47.2 all-gather.4
  83.7 72.6 all-gather.6
  158.6 91.2 all-gather.8
  304.8 40.3 reduce-scatter.3
  358.6 58.2 all-reduce.1
  419.3 45.8 all-gather.10
where the time goes:
time: 488 us; the launch traced here: 485 us
  waiting for transfers between devices  358 us (73%)
  matrix products  54 us (11%)
  other arithmetic  30.4 us (6%)
  local copies, waits for them, and re-layouts  23.6 us (5%)
  between operations  13.7 us (3%)
  starting transfers between devices  5.74 us (1%)
    all_gather x1, waiting for transfers between devices, local(): lax.all_gather(value_rows, 'ctx', axis=1, tiled=True)  93.5 us
    all_gather x1, waiting for transfers between devices, local(): lax.all_gather(key_rows, 'ctx', axis=1, tiled=True)  70.3 us
    psum x1, waiting for transfers between devices, local(): lax.psum(partial_value.astype(jnp.bfloat16), 'head').astype(jnp.float32)  58.4 us
    all_gather x1, waiting for transfers between devices, local(): lax.all_gather(trunk_out, 'head', axis=2, tiled=True)  47.3 us
    unnamed x7, waiting for transfers between devices  40.3 us
    all_gather x1, waiting for transfers between devices, local(): lax.all_gather(pair_proj[:, :, C:].astype(jnp.bfloat16), 'ctx', axis=1, t...  37.5 us
    dot_general x8, matrix products, attend_block(): jnp.einsum('vhqk,vkhe->vhqe', weights.astype(jnp.bfloat16), value_rows, p...  19.3 us
    dot_general x8, matrix products, attend_block(): jnp.einsum('vqhe,vkhe->vhqk', queries, key_rows, preferred_element_type=j...  14.5 us
  transfers between devices with their start and end apart: 8, of which 8 were waited for; matrix products, arithmetic and copies ran while one was open for 2% of the time, Pallas kernels for 0%

commit v1 on v0

v1 whole, which is shorter than its diff:
```python
import functools
import math

import jax
import jax.numpy as jnp
from jax import lax
from jax.experimental import pallas as pl
from jax.experimental.pallas import tpu as pltpu
from jax.sharding import PartitionSpec as P

HD = 128
VD = 192
C = 128
NB = 16
POOL = 4
DIL = 256
DEL = 128
SEGS = 3
BIG = -1e30
QSCALE = math.log2(math.e) / math.sqrt(HD)


def changed(delta, length):
    hit = jnp.logical_and(delta >= 0, delta < length)
    for shift in (-DIL, DIL):
        moved = delta + shift
        hit = jnp.logical_or(hit, jnp.logical_and(moved >= 0, moved < length))
    return hit


def attention_kernel(dels, q_ref, kv_ref, mod_ref, mix_ref, out_ref, k_aug, v_aug, m_aug, mv_aug):
    tokens = q_ref.shape[0]
    total = kv_ref.shape[0]
    variants = dels.shape[0]
    per = mod_ref.shape[0] // variants
    lane = lax.broadcasted_iota(jnp.int32, (1, 128), 1)
    first = jnp.zeros((1, 128), jnp.int32)
    length = jnp.zeros((1, 128), jnp.int32)
    for v in range(variants):
        first = jnp.where(lane == v, dels[v, 0], first)
        length = jnp.where(lane == v, dels[v, 1] - dels[v, 0], length)
    ones = jnp.where(lax.broadcasted_iota(jnp.int32, (1, 64), 1) == 0, 1.0, 0.0).astype(jnp.bfloat16)
    k_aug[:, :HD] = kv_ref[:, :HD]
    pos = lax.broadcasted_iota(jnp.int32, (total, 128), 0)
    k_aug[:, HD:] = jnp.where(changed(pos - first, length), BIG, 0.0).astype(jnp.bfloat16)
    v_aug[:, :VD] = kv_ref[:, HD:]
    v_aug[:, VD:] = jnp.broadcast_to(ones, (total, 64))
    m_aug[:, :HD] = mod_ref[:, HD : 2 * HD]
    mv_aug[:, :VD] = mod_ref[:, 2 * HD :]
    mv_aug[:, VD:] = jnp.broadcast_to(ones, (variants * per, 64))
    row = lax.broadcasted_iota(jnp.int32, (per, 128), 0)
    half = row // (per // 2)
    seg = (row % (per // 2)) // (DEL // 2)
    step = half * (DEL // 2) + row % (DEL // 2)
    for v in range(variants):
        token = dels[v, 0] + (seg - 1) * DIL + step
        valid = (step < dels[v, 1] - dels[v, 0]) & (token >= 0) & (token < total)
        m_aug[v * per : (v + 1) * per, HD:] = jnp.where(valid, 0.0, BIG).astype(jnp.bfloat16)

    start = lax.axis_index("ctx") * tokens
    col = lax.broadcasted_iota(jnp.int32, (tokens, per), 1)
    qpos = lax.broadcasted_iota(jnp.int32, (tokens, per), 0) + start
    col_half = col // (per // 2)
    col_seg = (col % (per // 2)) // (DEL // 2)
    col_step = col_half * (DEL // 2) + col % (DEL // 2)
    pool = (
        lax.broadcasted_iota(jnp.int32, (tokens // POOL, tokens), 1) // POOL
        == lax.broadcasted_iota(jnp.int32, (tokens // POOL, tokens), 0)
    ).astype(jnp.bfloat16)
    tile = 1024

    def one(v, _):
        s0 = dels[v, 0]
        ln = dels[v, 1] - s0
        place = jnp.logical_and(qpos == s0 + (col_seg - 1) * DIL + col_step, col_step < ln)
        moved = jnp.dot(
            place.astype(jnp.bfloat16),
            mod_ref[pl.ds(pl.multiple_of(v * per, per), per), :HD],
            preferred_element_type=jnp.float32,
        )
        is_mod = changed(qpos[:, :128] - s0, ln)
        queries = jnp.where(is_mod, moved, q_ref[...].astype(jnp.float32)).astype(jnp.bfloat16)
        pick = jnp.broadcast_to(jnp.where(lane == v, 1.0, 0.0), (tokens, 128)).astype(jnp.bfloat16)
        q_aug = jnp.concatenate([queries, pick], axis=1)
        top = jnp.full((tokens, 1), -3e38, jnp.float32)
        acc = jnp.zeros((tokens, 256), jnp.float32)

        def step_on(keys, values, top, acc):
            s = lax.dot_general(q_aug, keys, (((1,), (1,)), ((), ())), preferred_element_type=jnp.float32)
            new = jnp.maximum(top, s.max(1, keepdims=True))
            w = jnp.exp2(s - new).astype(jnp.bfloat16)
            acc = acc * jnp.exp2(top - new) + jnp.dot(w, values, preferred_element_type=jnp.float32)
            return new, acc

        for t in range(total // tile):
            rows = slice(t * tile, (t + 1) * tile)
            top, acc = step_on(k_aug[rows], v_aug[rows], top, acc)
        rows = pl.ds(pl.multiple_of(v * per, per), per)
        top, acc = step_on(m_aug[rows], mv_aug[rows], top, acc)
        out = (acc[:, :VD] / acc[:, VD : VD + 1]).astype(jnp.bfloat16)
        pooled = jnp.dot(pool, out, preferred_element_type=jnp.float32) * (1.0 / POOL)
        out_ref[v] = jnp.dot(pooled.astype(jnp.bfloat16), mix_ref[...], preferred_element_type=jnp.float32)
        return 0

    lax.fori_loop(0, variants, one, 0)


def attention(deletions, queries, kv, mod, mix):
    variants = deletions.shape[0]
    tokens = queries.shape[0]
    total = kv.shape[0]
    vm = pl.BlockSpec(memory_space=pltpu.VMEM)
    return pl.pallas_call(
        attention_kernel,
        out_shape=jax.ShapeDtypeStruct((variants, tokens // POOL, 2 * C), jnp.float32),
        in_specs=[pl.BlockSpec(memory_space=pltpu.SMEM), vm, vm, vm, vm],
        out_specs=vm,
        scratch_shapes=[
            pltpu.VMEM((total, 2 * HD), jnp.bfloat16),
            pltpu.VMEM((total, 256), jnp.bfloat16),
            pltpu.VMEM((mod.shape[0], 2 * HD), jnp.bfloat16),
            pltpu.VMEM((mod.shape[0], 256), jnp.bfloat16),
        ],
        compiler_params=pltpu.CompilerParams(vmem_limit_bytes=56 * 2**20),
    )(deletions, queries, kv, mod, mix)


def pair_kernel(rows_per, row_ref, col_ref, table_ref, out_ref, rel):
    step = pl.program_id(0)
    span = col_ref.shape[1]
    row_count = row_ref.shape[1]

    @pl.when(step == 0)
    def _():
        base = lax.axis_index("head") * span - lax.axis_index("ctx") * row_count - (row_count - 1)
        dist = jnp.abs(lax.broadcasted_iota(jnp.int32, rel.shape, 0) + base)
        value = jnp.broadcast_to(table_ref[0:1, :], rel.shape)
        for k in range(NB - 1):
            value = jnp.where(dist >= 2**k, table_ref[k + 1 : k + 2, :], value)
        rel[...] = value

    def one(i, _):
        row = step * rows_per + i
        shifted = rel[pl.ds(row_count - 1 - row, span), :]
        for v in range(row_ref.shape[0]):
            out_ref[v, i] = (row_ref[v, pl.ds(row, 1), :] + (col_ref[v] + shifted)).astype(out_ref.dtype)
        return 0

    lax.fori_loop(0, rows_per, one, 0)


def pair_map(row_feats, col_feats, table):
    variants, rows, _ = row_feats.shape
    cols = col_feats.shape[1]
    per = 8
    vm = pl.BlockSpec(memory_space=pltpu.VMEM)
    return pl.pallas_call(
        functools.partial(pair_kernel, per),
        grid=(rows // per,),
        out_shape=jax.ShapeDtypeStruct((variants, rows, cols, C), jnp.bfloat16),
        in_specs=[vm, vm, vm],
        out_specs=pl.BlockSpec((variants, per, cols, C), lambda i: (0, i, 0, 0)),
        scratch_shapes=[pltpu.VMEM((rows + cols, C), jnp.float32)],
        compiler_params=pltpu.CompilerParams(vmem_limit_bytes=32 * 2**20),
    )(row_feats, col_feats, table)


def local(sequence, deletions, conv_taps, conv_bias, w_proj, w_out, w_pair, dist_table):
    tokens, width = sequence.shape
    variants = deletions.shape[0]
    ctx = lax.axis_index("ctx")
    n_ctx = lax.axis_size("ctx")
    forward = [(i, i + 1) for i in range(n_ctx - 1)]
    backward = [(b, a) for a, b in forward]
    low = lax.ppermute(sequence[tokens - DIL :], "ctx", forward)
    high = lax.ppermute(sequence[:DIL], "ctx", backward)
    pair_weights = lax.all_gather(w_pair, "head", axis=0, tiled=True)
    mix = jnp.dot(w_out, pair_weights, preferred_element_type=jnp.float32).astype(jnp.bfloat16)

    ext = jnp.concatenate([low, sequence, high], 0)
    start = ctx * tokens
    pos = start - DIL + jnp.arange(tokens + 2 * DIL, dtype=jnp.int32)
    dels = jnp.concatenate([deletions, jnp.zeros((1, 2), jnp.int32)], 0)
    kept = jnp.logical_or(pos[None] < dels[:, :1], pos[None] >= dels[:, 1:])
    masked = jnp.where(kept[:, :, None], ext[None], jnp.zeros((), jnp.bfloat16)).astype(jnp.float32)
    conv = (
        conv_taps[0] * masked[:, :tokens]
        + conv_taps[1] * masked[:, DIL : DIL + tokens]
        + conv_taps[2] * masked[:, 2 * DIL :]
        + conv_bias
    )
    trunk = (masked[:, DIL : DIL + tokens] + jax.nn.gelu(conv, approximate=True)).astype(jnp.bfloat16)
    base, own = trunk[variants], trunk[:variants]
    pooled = own.astype(jnp.float32).reshape(variants, tokens // POOL, POOL, width).mean(2).astype(jnp.bfloat16)

    per = SEGS * DEL
    r = jnp.arange(per, dtype=jnp.int32)
    offset = ((r % (per // 2)) // (DEL // 2) - 1) * DIL + (r // (per // 2)) * (DEL // 2) + r % (DEL // 2)
    token = deletions[:, :1] + offset[None]
    pick = (token[:, :, None] == (start + jnp.arange(tokens, dtype=jnp.int32))[None, None]).astype(jnp.bfloat16)
    moved = jnp.einsum("vrt,vtd->vrd", pick, own, preferred_element_type=jnp.float32).astype(jnp.bfloat16)
    share = variants * per // n_ctx
    mod = lax.psum_scatter(moved.reshape(variants * per, width), "ctx", scatter_dimension=0, tiled=True)
    rows = lax.all_gather(jnp.concatenate([base, mod], 0), "head", axis=1, tiled=True)
    proj = jnp.dot(rows, w_proj, preferred_element_type=jnp.float32)
    proj = jnp.concatenate([proj[:, :HD] * QSCALE, proj[:, HD:]], 1).astype(jnp.bfloat16)
    kv = lax.all_gather(proj[:tokens, HD:], "ctx", axis=0, tiled=True)
    mod_all = lax.all_gather(proj[tokens:], "ctx", axis=0, tiled=True)
    part = attention(deletions, proj[:tokens, :HD], kv, mod_all, mix)
    part = part + jnp.einsum("vpd,dc->vpc", pooled, w_pair, preferred_element_type=jnp.float32)
    pair = lax.psum(part.astype(jnp.bfloat16), "head")
    cols = lax.all_gather(pair[:, :, C:], "ctx", axis=1, tiled=True)
    count = cols.shape[1] // lax.axis_size("head")
    cols = lax.dynamic_slice_in_dim(cols, lax.axis_index("head") * count, count, 1)
    return pair_map(pair[:, :, :C].astype(jnp.float32), cols.astype(jnp.float32), dist_table)


def solution(mesh):
    in_specs = (
        P("ctx", "head"),
        P("var", None),
        P(None, "head"),
        P("head"),
        P(None, "head"),
        P("head", None),
        P("head", None),
        P(),
    )
    out_specs = P("var", "ctx", "head", None)
    return jax.shard_map(local, mesh=mesh, in_specs=in_specs, out_specs=out_specs, check_vma=False)
```

time: 488 us -> 391 us (0.80)
  waiting for transfers between devices: 358 us -> 295 us
  matrix products: 54 us -> 8.08 us
  Pallas kernels: 0 us -> 30.6 us
  other arithmetic: 30.4 us -> 9.69 us
  blocking collectives: 0 us -> 13.6 us
  local copies, waits for them, and re-layouts: 23.6 us -> 12.8 us
    all_gather x4, waiting for transfers between devices: 249 us -> 162 us  [the longest x1 63.8 us: local(): kv = lax.all_gather(proj[:tokens, HD:], 'ctx', axis=0, tiled=True)]
    dot_general x19 -> x3, matrix products: 53.1 us -> 6.05 us  [the longest x1 3.24 us: local(): proj = jnp.dot(rows, w_proj, preferred_element_type=jnp.float32)]
    unnamed x7, waiting for transfers between devices: 40.3 us -> 75.5 us
    pallas_call x0 -> x2, Pallas kernels: none -> 30.6 us  [the longest x1 20.5 us: attention(): pl.pallas_call(attention_kernel, out_shape=jax.ShapeDtypeStruct((variants...]
    all_gather x0 -> x1, blocking collectives: none -> 13.6 us  [local(): pair_weights = lax.all_gather(w_pair, 'head', axis=0, tiled=True)]
    convert_element_type x5 -> x3, other arithmetic: 15.9 us -> 2.66 us  [the longest x1 1.47 us: local(): (masked[:, DIL:DIL + tokens] + jax.nn.gelu(conv, approximate=True)).astyp...]
    unnamed x24 -> x17, local copies, waits for them, and re-layouts: 14 us -> 3.85 us
    ppermute x2, waiting for transfers between devices: 10.2 us -> 1.61 us  [the longest x1 1.6 us: local(): high = lax.ppermute(sequence[:DIL], 'ctx', backward)]
  transfers between devices with their start and end apart: 8 -> 8, of which waited for: 8 -> 7; matrix products, arithmetic and copies ran while one was open for 2% -> 3% of each run, Pallas kernels for 0% -> 0%
where the time goes in v1:
time: 391 us; the launch traced here: 389 us
  waiting for transfers between devices  295 us (75%)
  Pallas kernels  30.6 us (8%)
  between operations  13.7 us (4%)
  blocking collectives  13.6 us (3%)
  local copies, waits for them, and re-layouts  12.8 us (3%)
  other arithmetic  9.69 us (2%)
  matrix products  8.08 us (2%)
  starting transfers between devices  5.54 us (1%)
    unnamed x7, waiting for transfers between devices  75.5 us
    all_gather x1, waiting for transfers between devices, local(): kv = lax.all_gather(proj[:tokens, HD:], 'ctx', axis=0, tiled=True)  63.8 us
    psum x1, waiting for transfers between devices, local(): pair = lax.psum(part.astype(jnp.bfloat16), 'head')  56.4 us
    all_gather x1, waiting for transfers between devices, local(): cols = lax.all_gather(pair[:, :, C:], 'ctx', axis=1, tiled=True)  46.3 us
    all_gather x1, waiting for transfers between devices, local(): lax.all_gather(jnp.concatenate([base, mod], 0), 'head', axis=1, tiled=True)  27.3 us
    all_gather x1, waiting for transfers between devices, local(): mod_all = lax.all_gather(proj[tokens:], 'ctx', axis=0, tiled=True)  24.3 us
    pallas_call x1, Pallas kernels, attention(): pl.pallas_call(attention_kernel, out_shape=jax.ShapeDtypeStruct((variants...  20.5 us
    all_gather x1, blocking collectives, local(): pair_weights = lax.all_gather(w_pair, 'head', axis=0, tiled=True)  13.6 us
  transfers between devices with their start and end apart: 8, of which 7 were waited for; matrix products, arithmetic and copies ran while one was open for 3% of the time, Pallas kernels for 0%

profile of v1, /device:TPU:1, one launch (start us, length us, event | category | flops | bytes accessed | tf_op | source)
XLA Modules:
  0.0 389.4 jit_solution(10533025652449614408)
XLA Ops:
  6.5 1.1 fusion.47
  7.6 4.0 %collective-permute-start = (bf16[256,192]{0,1:T(8,128)(2,1)S(1)}, bf16[256,192]{0,1:T(8,128)(2,1)S(1)}, u32[]{:S(2)}, u32[]{:S(2)}) collective-permute-start(bf16[256,192]{0,1:T(8,128)(2,1)S(1)} %get-tuple-element.7), channel_id=1, source_target_pairs={{0,16},{16,32},{32,48},{48,64},{64,80},{80,96},{96,112},{1,17},{17... | collective-permute-start | bytes 294920 | tf_op jit(solution)/shard_map/ppermute | solution.py:175
  11.6 1.3 collective-permute-start.1
  15.4 1.6 collective-permute-done.1
  18.7 1.5 fusion.10
  20.9 1.2 copy.38
  22.2 75.5 %reduce-scatter.4.cloned.1.call-done = bf16[192,192]{1,0:T(8,128)(2,1)} async-done(((bf16[1536,192]{1,0:T(8,128)(2,1)}), bf16[192,192]{1,0:T(8,128)(2,1)}) %reduce-scatter.4.cloned.1.call-update) | async-done | bytes 73744
  99.4 27.3 %all-gather.5.cloned.1.call-done = bf16[704,1536]{0,1:T(8,128)(2,1)} async-done(((bf16[704,192]{0,1:T(8,128)(2,1)}), bf16[704,1536]{0,1:T(8,128)(2,1)}) %all-gather.5.cloned.1.call-update) | async-done | bytes 2162704 | tf_op jit(solution)/shard_map/all_gather | solution.py:204
  126.7 3.2 fusion.49
  133.1 13.6 %all_gather.18 = bf16[1536,256]{1,0:T(8,128)(2,1)S(1)} all-gather(bf16[192,256]{1,0:T(8,128)(2,1)S(1)} %copy-done.3), channel_id=1, replica_groups=mesh['ctx'=8,'head'=8,'var'=2] {'head'}, dimensions={0}, use_global_device_ids=true | all-gather | bytes 884736 | tf_op jit(solution)/shard_map/all_gather | solution.py:177
  146.7 2.0 convolution_convert_fusion.mix_ref
  148.8 1.4 slice_convert_fusion
  150.1 2.0 copy.33
  152.1 1.4 bitcast_reduce_fusion
  153.5 1.2 copy.34
  154.7 1.6 slice.100.q_ref
  156.3 24.3 %all-gather.9.cloned.1.call-done.mod_ref = bf16[1536,448]{1,0:T(8,128)(2,1)} async-done(((bf16[192,448]{1,0:T(8,128)(2,1)}), bf16[1536,448]{1,0:T(8,128)(2,1)}) %all-gather.9.cloned.1.call-update) | async-done | bytes 1376272 | tf_op jit(solution)/shard_map/all_gather | solution.py:208
  180.6 63.8 %all-gather.7.cloned.1.call-done.kv_ref = bf16[4096,320]{1,0:T(8,128)(2,1)} async-done(((bf16[512,320]{1,0:T(8,128)(2,1)}), bf16[4096,320]{1,0:T(8,128)(2,1)}) %all-gather.7.cloned.1.call-update) | async-done | bytes 2621456 | tf_op jit(solution)/shard_map/all_gather | solution.py:207
  244.5 20.5 %shard_map.82 = f32[4,128,256]{2,1,0:T(8,128)} custom-call(s32[4,2]{1,0:T(4,128)} %copy.32.dels, bf16[512,128]{1,0:T(8,128)(2,1)} %slice.100.q_ref, bf16[4096,320]{1,0:T(8,128)(2,1)} %all-gather.7.cloned.1.call-done.kv_ref, bf16[1536,448]{1,0:T(8,128)(2,1)} %all-gather.9.cloned.1.call-done.mod_ref, bf16[192,256]{1,0:T(8,128)(2,1)} %convolution_convert_fusion.mix_ref), custom_call_target="tpu_custom_call" | custom-call | tf_op jit(solution)/shard_map/pallas_call | solution.py:113
  264.9 2.0 fusion.19
  267.0 56.4 %all-reduce.3.cloned.1.call-done = bf16[4,128,256]{2,1,0:T(8,128)(2,1)} async-done(((bf16[4,128,256]{2,1,0:T(8,128)(2,1)}), bf16[4,128,256]{2,1,0:T(8,128)(2,1)}) %all-reduce.3.cloned.1.call-update) | async-done | bytes 262160 | tf_op jit(solution)/shard_map/psum | solution.py:211
  323.4 1.6 fusion.46
  325.1 46.3 %all-gather.11.cloned.1.call-done = bf16[4,1024,128]{2,1,0:T(8,128)(2,1)} async-done(((bf16[4,128,128]{2,1,0:T(8,128)(2,1)}), bf16[4,1024,128]{2,1,0:T(8,128)(2,1)}) %all-gather.11.cloned.1.call-update) | async-done | bytes 1048592 | tf_op jit(solution)/shard_map/all_gather | solution.py:212
  372.4 10.1 %shard_map.83 = bf16[4,128,128,128]{3,2,1,0:T(8,128)(2,1)} custom-call(f32[4,128,128]{2,1,0:T(8,128)S(1)} %get-tuple-element.6.row_ref, f32[4,128,128]{2,1,0:T(8,128)S(1)} %dynamic-slice_convert_fusion.col_ref, f32[16,128]{1,0:T(8,128)S(1)} %copy-done.1), custom_call_target="tpu_custom_call" | custom-call | tf_op jit(solution)/shard_map/pallas_call | solution.py:157
  (47 shorter events, 10.7 us)
Async XLA Ops:
  6.5 120.2 %copy-start = (bf16[1536,448]{0,1:T(8,128)(2,1)S(1)}, bf16[1536,448]{0,1:T(8,128)(2,1)}, u32[]{:S(2)}) copy-start(bf16[1536,448]{0,1:T(8,128)(2,1)} %param.12) | copy-start | bytes 4128772
  6.5 91.1 %reduce-scatter.4.cloned.1.call-start = ((), (), s32[]{:S(2)}) async-start(), calls=%async_computation.6 | async-start | bytes 884736
  7.6 7.8 %collective-permute-start = (bf16[256,192]{0,1:T(8,128)(2,1)S(1)}, bf16[256,192]{0,1:T(8,128)(2,1)S(1)}, u32[]{:S(2)}, u32[]{:S(2)}) collective-permute-start(bf16[256,192]{0,1:T(8,128)(2,1)S(1)} %get-tuple-element.7), channel_id=1, source_target_pairs={{0,16},{16,32},{32,48},{48,64},{64,80},{80,96},{96,112},{1,17},{17... | collective-permute-start | bytes 294920 | tf_op jit(solution)/shard_map/ppermute | solution.py:175
  11.6 5.4 %collective-permute-start.1 = (bf16[256,192]{0,1:T(8,128)(2,1)S(1)}, bf16[256,192]{0,1:T(8,128)(2,1)S(1)}, u32[]{:S(2)}, u32[]{:S(2)}) collective-permute-start(bf16[256,192]{0,1:T(8,128)(2,1)S(1)} %get-tuple-element.8), channel_id=1, source_target_pairs={{16,0},{32,16},{48,32},{64,48},{80,64},{96,80},{112,96},{17,1},{33... | collective-permute-start | bytes 294920 | tf_op jit(solution)/shard_map/ppermute | solution.py:176
  18.0 0.7 copy-start.6
  22.1 104.6 %all-gather.5.cloned.1.call-start = ((), (), s32[]{:S(2)}) async-start(), calls=%async_computation.1 | async-start | bytes 2654208 | tf_op jit(solution)/shard_map/all_gather | solution.py:204
  99.4 81.2 %all-gather.9.cloned.1.call-start = ((), (), s32[]{:S(2)}) async-start(), calls=%async_computation.3 | async-start | bytes 1769472 | tf_op jit(solution)/shard_map/all_gather | solution.py:208
  130.0 2.4 copy-start.5
  130.0 3.1 copy-start.3
  130.1 0.7 copy-start.2
  131.5 113.0 %all-gather.7.cloned.1.call-start = ((), (), s32[]{:S(2)}) async-start(), calls=%async_computation.2 | async-start | bytes 3538944 | tf_op jit(solution)/shard_map/all_gather | solution.py:207
  132.4 191.1 %all-reduce.3.cloned.1.call-start = ((), (), s32[]{:S(2)}) async-start(), calls=%async_computation.4 | async-start | bytes 524288 | tf_op jit(solution)/shard_map/psum | solution.py:211
  156.3 108.6 %copy-start.4 = (bf16[192,256]{1,0:T(8,128)(2,1)S(1)}, bf16[192,256]{1,0:T(8,128)(2,1)}, u32[]{:S(2)}) copy-start(bf16[192,256]{1,0:T(8,128)(2,1)} %param.14) | copy-start | bytes 294916
  264.9 107.5 %copy-start.1 = (f32[16,128]{1,0:T(8,128)S(1)}, f32[16,128]{1,0:T(8,128)}, u32[]{:S(2)}) copy-start(f32[16,128]{1,0:T(8,128)} %table_ref.1) | copy-start | bytes 24580
  267.0 104.5 %all-gather.11.cloned.1.call-start = ((), (), s32[]{:S(2)}) async-start(), calls=%async_computation.5 | async-start | bytes 1179648 | tf_op jit(solution)/shard_map/all_gather | solution.py:212
Sparse Core Ops, SparseCore 0:
  22.2 75.3 reduce-scatter.3
  99.5 27.1 all-gather.4
  131.6 48.9 all-gather.8
  183.0 61.3 all-gather.6
  267.1 56.2 all-reduce.2
  325.6 45.8 all-gather.10

commit v2 on v1

v2 whole, which is shorter than its diff:
```python
import functools
import math

import jax
import jax.numpy as jnp
from jax import lax
from jax.experimental import pallas as pl
from jax.experimental.pallas import tpu as pltpu
from jax.sharding import PartitionSpec as P

HD = 128
VD = 192
C = 128
NB = 16
POOL = 4
DIL = 256
DEL = 128
SEGS = 3
BIG = -1e30
QSCALE = math.log2(math.e) / math.sqrt(HD)


def changed(delta, length):
    hit = jnp.logical_and(delta >= 0, delta < length)
    for shift in (-DIL, DIL):
        moved = delta + shift
        hit = jnp.logical_or(hit, jnp.logical_and(moved >= 0, moved < length))
    return hit


def attention_kernel(dels, q_ref, kv_ref, mod_ref, mix_ref, pooled_ref, wp_ref, out_ref, k_aug, v_aug, m_aug, mv_aug, mq):
    tokens = q_ref.shape[0]
    blocks = kv_ref.shape[0]
    total = tokens * blocks
    variants = dels.shape[0]
    share = SEGS * DEL // 2
    per = 2 * share
    lane = lax.broadcasted_iota(jnp.int32, (1, 128), 1)
    first = jnp.zeros((1, 128), jnp.int32)
    length = jnp.zeros((1, 128), jnp.int32)
    for v in range(variants):
        first = jnp.where(lane == v, dels[v, 0], first)
        length = jnp.where(lane == v, dels[v, 1] - dels[v, 0], length)
    one_lane = jnp.where(lane == VD - 128, 1.0, 0.0).astype(jnp.bfloat16)

    def spread(tail):
        both = jnp.concatenate([tail, jnp.concatenate([tail[:, 64:], tail[:, :64]], axis=1)], axis=0)
        keep = lax.broadcasted_iota(jnp.int32, both.shape, 1) < VD - 128
        return jnp.where(keep, both, jnp.broadcast_to(one_lane, both.shape))

    for b in range(blocks):
        rows = slice(b * tokens, (b + 1) * tokens)
        k_aug[rows, :HD] = kv_ref[b, :tokens]
        v_aug[rows, :128] = kv_ref[b, tokens : 2 * tokens]
        v_aug[rows, 128:] = spread(kv_ref[b, 2 * tokens :])
        pos = lax.broadcasted_iota(jnp.int32, (tokens, 128), 0) + b * tokens
        k_aug[rows, HD:] = jnp.where(changed(pos - first, length), BIG, 0.0).astype(jnp.bfloat16)
        rows = slice(b * share, (b + 1) * share)
        mq[rows] = mod_ref[b, :share]
        m_aug[rows, :HD] = mod_ref[b, share : 2 * share]
        mv_aug[rows, :128] = mod_ref[b, 2 * share : 3 * share]
        mv_aug[rows, 128:] = spread(mod_ref[b, 3 * share :])
    row = lax.broadcasted_iota(jnp.int32, (per, 128), 0)
    half = row // (per // 2)
    seg = (row % (per // 2)) // (DEL // 2)
    step = half * (DEL // 2) + row % (DEL // 2)
    for v in range(variants):
        token = dels[v, 0] + (seg - 1) * DIL + step
        valid = (step < dels[v, 1] - dels[v, 0]) & (token >= 0) & (token < total)
        m_aug[v * per : (v + 1) * per, HD:] = jnp.where(valid, 0.0, BIG).astype(jnp.bfloat16)

    start = lax.axis_index("ctx") * tokens
    col = lax.broadcasted_iota(jnp.int32, (tokens, per), 1)
    qpos = lax.broadcasted_iota(jnp.int32, (tokens, per), 0) + start
    col_half = col // (per // 2)
    col_seg = (col % (per // 2)) // (DEL // 2)
    col_step = col_half * (DEL // 2) + col % (DEL // 2)
    pool = (
        lax.broadcasted_iota(jnp.int32, (tokens // POOL, tokens), 1) // POOL
        == lax.broadcasted_iota(jnp.int32, (tokens // POOL, tokens), 0)
    ).astype(jnp.bfloat16)
    tile = 1024

    def one(v, _):
        s0 = dels[v, 0]
        ln = dels[v, 1] - s0
        place = jnp.logical_and(qpos == s0 + (col_seg - 1) * DIL + col_step, col_step < ln)
        moved = jnp.dot(
            place.astype(jnp.bfloat16),
            mq[pl.ds(pl.multiple_of(v * per, per), per), :],
            preferred_element_type=jnp.float32,
        )
        is_mod = changed(qpos[:, :128] - s0, ln)
        queries = jnp.where(is_mod, moved, q_ref[...].astype(jnp.float32)).astype(jnp.bfloat16)
        pick = jnp.broadcast_to(jnp.where(lane == v, 1.0, 0.0), (tokens, 128)).astype(jnp.bfloat16)
        q_aug = jnp.concatenate([queries, pick], axis=1)
        top = jnp.full((tokens, 1), -3e38, jnp.float32)
        acc = jnp.zeros((tokens, 256), jnp.float32)

        def step_on(keys, values, top, acc):
            s = lax.dot_general(q_aug, keys, (((1,), (1,)), ((), ())), preferred_element_type=jnp.float32)
            new = jnp.maximum(top, s.max(1, keepdims=True))
            w = jnp.exp2(s - new).astype(jnp.bfloat16)
            acc = acc * jnp.exp2(top - new) + jnp.dot(w, values, preferred_element_type=jnp.float32)
            return new, acc

        for t in range(total // tile):
            rows = slice(t * tile, (t + 1) * tile)
            top, acc = step_on(k_aug[rows], v_aug[rows], top, acc)
        rows = pl.ds(pl.multiple_of(v * per, per), per)
        top, acc = step_on(m_aug[rows], mv_aug[rows], top, acc)
        out = (acc[:, :VD] / acc[:, VD : VD + 1]).astype(jnp.bfloat16)
        pooled = jnp.dot(pool, out, preferred_element_type=jnp.float32) * (1.0 / POOL)
        out_ref[v] = jnp.dot(
            pooled.astype(jnp.bfloat16), mix_ref[...], preferred_element_type=jnp.float32
        ) + jnp.dot(pooled_ref[v], wp_ref[...], preferred_element_type=jnp.float32)
        return 0

    lax.fori_loop(0, variants, one, 0)


def attention(deletions, queries, kv, mod, mix, pooled, w_pair):
    variants = deletions.shape[0]
    tokens = queries.shape[0]
    total = kv.shape[0] * tokens
    changed_rows = variants * SEGS * DEL
    vm = pl.BlockSpec(memory_space=pltpu.VMEM)
    return pl.pallas_call(
        attention_kernel,
        out_shape=jax.ShapeDtypeStruct((variants, tokens // POOL, 2 * C), jnp.float32),
        in_specs=[pl.BlockSpec(memory_space=pltpu.SMEM)] + [vm] * 6,
        out_specs=vm,
        scratch_shapes=[
            pltpu.VMEM((total, 2 * HD), jnp.bfloat16),
            pltpu.VMEM((total, 256), jnp.bfloat16),
            pltpu.VMEM((changed_rows, 2 * HD), jnp.bfloat16),
            pltpu.VMEM((changed_rows, 256), jnp.bfloat16),
            pltpu.VMEM((changed_rows, HD), jnp.bfloat16),
        ],
        compiler_params=pltpu.CompilerParams(vmem_limit_bytes=56 * 2**20),
    )(deletions, queries, kv, mod, mix, pooled, w_pair)


def pair_kernel(rows_per, row_ref, col_ref, table_ref, out_ref, rel):
    step = pl.program_id(0)
    span = col_ref.shape[1]
    row_count = row_ref.shape[1]

    @pl.when(step == 0)
    def _():
        base = lax.axis_index("head") * span - lax.axis_index("ctx") * row_count - (row_count - 1)
        dist = jnp.abs(lax.broadcasted_iota(jnp.int32, rel.shape, 0) + base)
        value = jnp.broadcast_to(table_ref[0:1, :], rel.shape)
        for k in range(NB - 1):
            value = jnp.where(dist >= 2**k, table_ref[k + 1 : k + 2, :], value)
        rel[...] = value

    def one(i, _):
        row = step * rows_per + i
        shifted = rel[pl.ds(row_count - 1 - row, span), :]
        for v in range(row_ref.shape[0]):
            out_ref[v, i] = (row_ref[v, pl.ds(row, 1), :] + (col_ref[v] + shifted)).astype(out_ref.dtype)
        return 0

    lax.fori_loop(0, rows_per, one, 0)


def pair_map(row_feats, col_feats, table):
    variants, rows, _ = row_feats.shape
    cols = col_feats.shape[1]
    per = 8
    vm = pl.BlockSpec(memory_space=pltpu.VMEM)
    return pl.pallas_call(
        functools.partial(pair_kernel, per),
        grid=(rows // per,),
        out_shape=jax.ShapeDtypeStruct((variants, rows, cols, C), jnp.bfloat16),
        in_specs=[vm, vm, vm],
        out_specs=pl.BlockSpec((variants, per, cols, C), lambda i: (0, i, 0, 0)),
        scratch_shapes=[pltpu.VMEM((rows + cols, C), jnp.float32)],
        compiler_params=pltpu.CompilerParams(vmem_limit_bytes=32 * 2**20),
    )(row_feats, col_feats, table)


MESH = pl.DeviceIdType.MESH


def pack(x):
    half = x.shape[0] // 2
    tail = jnp.concatenate([x[:half, 128:], x[half:, 128:]], axis=1)
    return jnp.concatenate([x[:, :128], tail], axis=0)


class Ring:
    def __init__(self, make, buf, rows, base, me, dn, up, far, mate, mate_of, to_dn, to_up, to_mate):
        half = rows // 2
        self.full, self.lo, self.hi = pl.ds(0, rows), pl.ds(0, half), pl.ds(half, half)
        self.make, self.buf, self.base = make, buf, base
        self.me, self.dn, self.up, self.far, self.mate, self.mate_of = me, dn, up, far, mate, mate_of
        self.to_dn, self.to_up, self.to_mate = to_dn, to_up, to_mate
        self.sent = []

    def copy(self, slot, rows, index, target):
        ref = self.buf.at[slot, rows]
        return self.make(ref, ref, self.base + index, target)

    def send(self, slot, rows, index, target):
        made = self.copy(slot, rows, index, target)
        made.start()
        self.sent.append(made)

    def got(self, slot, rows, index):
        self.copy(slot, rows, index, self.to_up).wait_recv()


class HeadRing(Ring):
    def begin(self):
        self.send(self.me, self.full, 0, self.to_up)
        self.send(self.me, self.full, 1, self.to_dn)
        self.send(self.me, self.full, 2, self.to_mate)

    def relay(self):
        self.got(self.dn, self.full, 0)
        self.send(self.dn, self.lo, 3, self.to_up)
        self.send(self.dn, self.full, 4, self.to_mate)
        self.got(self.up, self.full, 1)
        self.send(self.up, self.hi, 5, self.to_dn)
        self.send(self.up, self.full, 6, self.to_mate)

    def end(self):
        self.got(self.far, self.lo, 3)
        self.send(self.far, self.lo, 7, self.to_mate)
        self.got(self.far, self.hi, 5)
        self.send(self.far, self.hi, 8, self.to_mate)
        self.got(self.mate, self.full, 2)
        self.got(self.mate_of(self.dn), self.full, 4)
        self.got(self.mate_of(self.up), self.full, 6)
        self.got(self.mate_of(self.far), self.lo, 7)
        self.got(self.mate_of(self.far), self.hi, 8)

    def drain(self):
        for made in self.sent:
            made.wait_send()


class TokenRing(Ring):
    def begin(self):
        self.send(self.me, self.full, 2, self.to_mate)
        self.send(self.me, self.full, 0, self.to_up)
        self.send(self.me, self.full, 1, self.to_dn)

    def cross(self):
        self.got(self.mate, self.full, 2)
        self.send(self.mate, self.full, 4, self.to_up)
        self.send(self.mate, self.full, 6, self.to_dn)

    def relay(self):
        self.got(self.dn, self.full, 0)
        self.send(self.dn, self.lo, 3, self.to_up)
        self.got(self.up, self.full, 1)
        self.send(self.up, self.hi, 5, self.to_dn)

    def relay_mate(self):
        dn, up = self.mate_of(self.dn), self.mate_of(self.up)
        self.got(dn, self.full, 4)
        self.send(dn, self.lo, 7, self.to_up)
        self.got(up, self.full, 6)
        self.send(up, self.hi, 8, self.to_dn)

    def end(self):
        self.got(self.far, self.lo, 3)
        self.got(self.far, self.hi, 5)
        self.got(self.mate_of(self.far), self.lo, 7)
        self.got(self.mate_of(self.far), self.hi, 8)

    def drain(self):
        for made in self.sent:
            made.wait_send()


def rows_kernel(dels, seq, taps, bias, w_ref, wo_ref, wp_ref,
                q_out, kv_out, mod_out, pooled_out, mix_out,
                low, high, gb, gm, wp, moved, landed, kv, mod, wb1, wb2, proj, projm, send, recv):
    tokens, width = seq.shape
    variants = dels.shape[0]
    c, h, g = lax.axis_index("ctx"), lax.axis_index("head"), lax.axis_index("var")
    n = 8
    dn_h, up_h, far_h = lax.rem(h + 6, n), lax.rem(h + 2, n), lax.rem(h + 4, n)
    sib = h + 1 - 2 * lax.rem(h, 2)
    x0, y0 = c // 4 * 4, lax.rem(c, 4)
    up_c, dn_c, far_c = x0 + lax.rem(y0 + 1, 4), x0 + lax.rem(y0 + 3, 4), x0 + lax.rem(y0 + 2, 4)
    xp = lax.rem(c + 4, n)
    other = lambda t: lax.rem(t + 4, n)
    sib_of = lambda t: t + 1 - 2 * lax.rem(t, 2)

    barrier = pltpu.get_barrier_semaphore()
    peers = [{"ctx": lax.rem(c + k, n)} for k in range(1, n)]
    peers += [{"head": dn_h}, {"head": up_h}, {"head": sib}, {"ctx": xp, "var": 1 - g}]
    for peer in peers:
        pl.semaphore_signal(barrier, inc=1, device_id=peer, device_id_type=MESH)
    pl.semaphore_wait(barrier, len(peers))

    def make(src, dst, index, target):
        return pltpu.make_async_remote_copy(
            src_ref=src, dst_ref=dst, send_sem=send.at[index], recv_sem=recv.at[index],
            device_id=target, device_id_type=MESH,
        )

    right, left = {"ctx": lax.rem(c + 1, n)}, {"ctx": lax.rem(c + 7, n)}
    halo_low = make(seq.at[pl.ds(tokens - DIL, DIL)], low, 0, right)
    halo_high = make(seq.at[pl.ds(0, DIL)], high, 1, left)
    halo_low.start()
    halo_high.start()

    def head_ring(buf, rows, base):
        return HeadRing(make, buf, rows, base, h, dn_h, up_h, far_h, sib, sib_of,
                        {"head": dn_h}, {"head": up_h}, {"head": sib})

    def token_ring(buf, rows, base, to_mate):
        return TokenRing(make, buf, rows, base, c, dn_c, up_c, far_c, xp, other,
                         {"ctx": dn_c}, {"ctx": up_c}, to_mate)

    ring_b = head_ring(gb, gb.shape[1], 10)
    ring_m = head_ring(gm, gm.shape[1], 20)
    ring_p = head_ring(wp, wp.shape[1], 30)
    ring_k = token_ring(kv, kv.shape[1], 40, {"ctx": xp, "var": 1 - g})
    ring_o = token_ring(mod, mod.shape[1], 50, {"ctx": xp})

    wp[h] = wp_ref[...]

    zero = jnp.zeros((64, w_ref.shape[1]), jnp.bfloat16)
    for k in range(n):
        part = w_ref[k * 192 + 128 : k * 192 + 192, :]
        wb1[k * 128 : k * 128 + 64, :] = part
        wb1[k * 128 + 64 : k * 128 + 128, :] = zero
        wb2[k * 128 : k * 128 + 64, :] = zero
        wb2[k * 128 + 64 : k * 128 + 128, :] = part

    halo_low.wait()
    halo_high.wait()
    pos = lax.broadcasted_iota(jnp.int32, (tokens, width), 0) + c * tokens
    tap0, tap1, tap2 = taps[0:1, :], taps[1:2, :], taps[2:3, :]

    def row_block(first, length, lo, hi):
        def masked(ref, begin, shift):
            x = ref[begin : begin + DIL].astype(jnp.float32)
            d = pos[lo:hi] + shift - first
            return jnp.where((d >= 0) & (d < length), 0.0, x)

        if lo == 0:
            before = jnp.where(c == 0, 0.0, masked(low, 0, -DIL))
            after = masked(seq, DIL, DIL)
        else:
            before = masked(seq, 0, -DIL)
            after = jnp.where(c == n - 1, 0.0, masked(high, 0, DIL))
        here = masked(seq, lo, 0)
        conv = tap0 * before + tap1 * here + tap2 * after + bias[...]
        return (here + jax.nn.gelu(conv, approximate=True)).astype(jnp.bfloat16)

    def trunk(first, length):
        return jnp.concatenate([row_block(first, length, 0, DIL), row_block(first, length, DIL, 2 * DIL)], axis=0)

    gb[h] = pack(trunk(0, 0))
    ring_b.begin()

    share = SEGS * DEL // 2
    r = lax.broadcasted_iota(jnp.int32, (share, tokens), 0)
    offset = (r // (DEL // 2) - 1) * DIL + r % (DEL // 2)
    here = lax.broadcasted_iota(jnp.int32, (share, tokens), 1) + c * tokens
    pool = (
        lax.broadcasted_iota(jnp.int32, (tokens // POOL, tokens), 1) // POOL
        == lax.broadcasted_iota(jnp.int32, (tokens // POOL, tokens), 0)
    ).astype(jnp.bfloat16)

    def variant(v, _):
        first = dels[v, 0]
        own = trunk(first, dels[v, 1] - first)
        for half in range(2):
            pick = (here == offset + (first + half * (DEL // 2))).astype(jnp.bfloat16)
            moved[2 * v + half] = pack(jnp.dot(pick, own, preferred_element_type=jnp.float32).astype(jnp.bfloat16))
        pooled_out[v] = (jnp.dot(pool, own, preferred_element_type=jnp.float32) * (1.0 / POOL)).astype(jnp.bfloat16)
        return 0

    lax.fori_loop(0, variants, variant, 0)
    shared = []
    for k in range(1, n):
        to = lax.rem(c + k, n)
        made = make(moved.at[to], landed.at[k - 1], 1 + k, {"ctx": to})
        made.start()
        shared.append(made)
    ring_p.begin()
    ring_b.relay()
    total = moved[c]
    for k in range(1, n):
        shared[k - 1].wait_recv()
        total = total + landed[k - 1]
    gm[h] = total
    ring_m.begin()
    ring_b.end()

    def project(buf, rows, out):
        half = rows // 2
        for k in range(0, n, 2):
            a = jnp.concatenate([buf[k, :rows, :], buf[k + 1, :rows, :]], axis=1)
            wa = jnp.concatenate([w_ref[k * 192 : k * 192 + 128, :], w_ref[k * 192 + 192 : k * 192 + 320, :]], axis=0)
            part = jnp.dot(a, wa, preferred_element_type=jnp.float32)
            b = jnp.concatenate([buf[k, rows : rows + half, :], buf[k + 1, rows : rows + half, :]], axis=1)
            top = jnp.dot(b, wb1[k * 128 : k * 128 + 256, :], preferred_element_type=jnp.float32)
            bot = jnp.dot(b, wb2[k * 128 : k * 128 + 256, :], preferred_element_type=jnp.float32)
            part = part + jnp.concatenate([top, bot], axis=0)
            if k == 0:
                out[...] = part
            else:
                out[...] += part

    project(gb, tokens, proj)
    kv[c, :tokens] = proj[:, HD : 2 * HD].astype(jnp.bfloat16)
    kv[c, tokens:] = pack(proj[:, 2 * HD :].astype(jnp.bfloat16))
    ring_k.begin()
    q_out[...] = (proj[:, :HD] * QSCALE).astype(jnp.bfloat16)
    ring_m.relay()
    ring_p.relay()
    ring_m.end()
    project(gm, share, projm)
    mod[c, :share] = (projm[:, :HD] * QSCALE).astype(jnp.bfloat16)
    mod[c, share : 2 * share] = projm[:, HD : 2 * HD].astype(jnp.bfloat16)
    mod[c, 2 * share :] = pack(projm[:, 2 * HD :].astype(jnp.bfloat16))
    ring_o.begin()
    ring_p.end()
    mix = jnp.zeros((wo_ref.shape[0], 2 * C), jnp.float32)
    for k in range(0, n, 2):
        wide = jnp.concatenate([wp[k], wp[k + 1]], axis=0)
        mix = mix + jnp.dot(wo_ref[:, k * 192 : k * 192 + 384], wide, preferred_element_type=jnp.float32)
    mix_out[...] = mix.astype(jnp.bfloat16)
    ring_k.cross()
    ring_k.relay()
    ring_o.cross()
    ring_o.relay()
    ring_k.relay_mate()
    ring_o.relay_mate()
    ring_k.end()
    ring_o.end()
    for ring in (ring_b, ring_m, ring_p, ring_k, ring_o):
        ring.drain()
    for made in shared:
        made.wait_send()
    kv_out[...] = kv[...]
    mod_out[...] = mod[...]


def project_rows(sequence, deletions, conv_taps, conv_bias, w_proj, w_out, w_pair):
    tokens, width = sequence.shape
    variants = deletions.shape[0]
    n = 8
    share = SEGS * DEL // 2
    vm = pl.BlockSpec(memory_space=pltpu.VMEM)
    bf = jnp.bfloat16
    kv_rows, mod_rows = tokens * 5 // 2, share * 7 // 2
    return pl.pallas_call(
        rows_kernel,
        out_shape=(
            jax.ShapeDtypeStruct((tokens, HD), bf),
            jax.ShapeDtypeStruct((n, kv_rows, 128), bf),
            jax.ShapeDtypeStruct((n, mod_rows, 128), bf),
            jax.ShapeDtypeStruct((variants, tokens // POOL, width), bf),
            jax.ShapeDtypeStruct((w_out.shape[0], 2 * C), bf),
        ),
        in_specs=[pl.BlockSpec(memory_space=pltpu.SMEM)] + [vm] * 6,
        out_specs=(vm,) * 5,
        scratch_shapes=[
            pltpu.VMEM((DIL, width), bf),
            pltpu.VMEM((DIL, width), bf),
            pltpu.VMEM((n, tokens * 3 // 2, 128), bf),
            pltpu.VMEM((n, share * 3 // 2, 128), bf),
            pltpu.VMEM((n, width, 2 * C), bf),
            pltpu.VMEM((n, share * 3 // 2, 128), bf),
            pltpu.VMEM((n - 1, share * 3 // 2, 128), bf),
            pltpu.VMEM((n, kv_rows, 128), bf),
            pltpu.VMEM((n, mod_rows, 128), bf),
            pltpu.VMEM((n * 128, w_proj.shape[1]), bf),
            pltpu.VMEM((n * 128, w_proj.shape[1]), bf),
            pltpu.VMEM((tokens, w_proj.shape[1]), jnp.float32),
            pltpu.VMEM((share, w_proj.shape[1]), jnp.float32),
            pltpu.SemaphoreType.DMA((60,)),
            pltpu.SemaphoreType.DMA((60,)),
        ],
        compiler_params=pltpu.CompilerParams(
            collective_id=0, has_side_effects=True, vmem_limit_bytes=56 * 2**20
        ),
    )(deletions, sequence, conv_taps, conv_bias.reshape(1, width), w_proj, w_out, w_pair)


def sum_kernel(part, row_out, col_out, mine, landed, rows_buf, cols_buf, feats, send, recv):
    c, h = lax.axis_index("ctx"), lax.axis_index("head")
    n = 8
    count = part.shape[0] // n
    on_diag = (c == h).astype(jnp.int32)
    barrier = pltpu.get_barrier_semaphore()
    for k in range(1, n):
        pl.semaphore_signal(barrier, inc=1, device_id={"head": lax.rem(h + k, n)}, device_id_type=MESH)
    for k in range(n):
        source = lax.rem(h + k, n)

        @pl.when(jnp.logical_or(c != h, k != 0))
        def _():
            pl.semaphore_signal(barrier, inc=1, device_id={"ctx": h, "head": source}, device_id_type=MESH)

    pl.semaphore_wait(barrier, (n - 1) + n - on_diag)

    def make(src, dst, index, target, arrival=None):
        return pltpu.make_async_remote_copy(
            src_ref=src, dst_ref=dst, send_sem=send.at[index],
            recv_sem=recv.at[index if arrival is None else arrival],
            device_id=target, device_id_type=MESH,
        )

    mine[...] = part[...].astype(jnp.bfloat16)
    first = []
    for k in range(1, n):
        to = lax.rem(h + k, n)
        made = make(mine.at[pl.ds(pl.multiple_of(to * count, count), count)], landed.at[k - 1], k, {"head": to})
        made.start()
        first.append(made)
    total = part[pl.ds(pl.multiple_of(h * count, count), count), :]
    for k in range(1, n):
        first[k - 1].wait_recv()
        total = total + landed[k - 1].astype(jnp.float32)
    feats[0] = total[:, :C].astype(jnp.bfloat16)
    feats[1] = total[:, C:].astype(jnp.bfloat16)
    rows_buf[h] = feats[0]
    for k in range(1, n):
        to = lax.rem(h + k, n)
        make(feats.at[0], rows_buf.at[h], n + k, {"head": to}).start()
    for k in range(n):
        to = lax.rem(c + k, n)

        @pl.when(jnp.logical_or(c != h, k != 0))
        def _():
            make(feats.at[1], cols_buf.at[h], 2 * n + k, {"ctx": to, "head": c}, 2 * n + h).start()

        @pl.when(jnp.logical_and(c == h, k == 0))
        def _():
            cols_buf[h] = feats[1]

    for k in range(1, n):
        source = lax.rem(h + n - k, n)
        made = make(feats.at[0], rows_buf.at[source], n + k, {"head": lax.rem(h + k, n)})
        made.wait_recv()
        made.wait_send()
    for k in range(n):
        @pl.when(jnp.logical_or(c != h, k != h))
        def _():
            make(feats.at[1], cols_buf.at[k], 2 * n + k, {"head": lax.rem(h + 1, n)}).wait_recv()

        @pl.when(jnp.logical_or(c != h, k != 0))
        def _():
            make(feats.at[1], cols_buf.at[h], 2 * n + k, {"head": lax.rem(h + 1, n)}).wait_send()
    for made in first:
        made.wait_send()
    for k in range(n):
        row_out[k * count : (k + 1) * count] = rows_buf[k].astype(jnp.float32)
        col_out[k * count : (k + 1) * count] = cols_buf[k].astype(jnp.float32)


def sum_heads(part):
    rows = part.shape[0]
    n = 8
    count = rows // n
    vm = pl.BlockSpec(memory_space=pltpu.VMEM)
    return pl.pallas_call(
        sum_kernel,
        out_shape=(jax.ShapeDtypeStruct((rows, C), jnp.float32),) * 2,
        in_specs=[vm],
        out_specs=(vm, vm),
        scratch_shapes=[
            pltpu.VMEM((rows, 2 * C), jnp.bfloat16),
            pltpu.VMEM((n - 1, count, 2 * C), jnp.bfloat16),
            pltpu.VMEM((n, count, C), jnp.bfloat16),
            pltpu.VMEM((n, count, C), jnp.bfloat16),
            pltpu.VMEM((2, count, C), jnp.bfloat16),
            pltpu.SemaphoreType.DMA((3 * n,)),
            pltpu.SemaphoreType.DMA((3 * n,)),
        ],
        compiler_params=pltpu.CompilerParams(collective_id=1, has_side_effects=True),
    )(part)


def local(sequence, deletions, conv_taps, conv_bias, w_proj, w_out, w_pair, dist_table):
    queries, kv, mod, pooled, mix = project_rows(
        sequence, deletions, conv_taps, conv_bias, w_proj, w_out, w_pair
    )
    part = attention(deletions, queries, kv, mod, mix, pooled, w_pair)
    variants, rows, _ = part.shape
    row_feats, col_feats = sum_heads(part.reshape(variants * rows, 2 * C))
    return pair_map(row_feats.reshape(variants, rows, C), col_feats.reshape(variants, rows, C), dist_table)


def solution(mesh):
    in_specs = (
        P("ctx", "head"),
        P("var", None),
        P(None, "head"),
        P("head"),
        P(None, "head"),
        P("head", None),
        P("head", None),
        P(),
    )
    out_specs = P("var", "ctx", "head", None)
    return jax.shard_map(local, mesh=mesh, in_specs=in_specs, out_specs=out_specs, check_vma=False)
```

time: 391 us -> 123 us (0.31)
  waiting for transfers between devices: 295 us -> 0 us
  Pallas kernels: 30.6 us -> 114 us
  between operations: 13.7 us -> 0.04 us
  blocking collectives: 13.6 us -> 0 us
  other arithmetic: 9.69 us -> 0 us
  matrix products: 8.08 us -> 0 us
  starting transfers between devices: 5.54 us -> 0 us
  local copies, waits for them, and re-layouts: 12.8 us -> 7.54 us
    all_gather x4 -> x0, waiting for transfers between devices: 162 us -> none  [the longest x1 63.8 us: local(): kv = lax.all_gather(proj[:tokens, HD:], 'ctx', axis=0, tiled=True)]
    pallas_call x0 -> x2, Pallas kernels: none -> 83.6 us  [the longest x1 68.3 us: project_rows(): pl.pallas_call(rows_kernel, out_shape=(jax.ShapeDtypeStruct((tokens, HD),...]
    unnamed x7 -> x0, waiting for transfers between devices: 75.5 us -> none
    psum x1 -> x0, waiting for transfers between devices: 56.4 us -> none  [local(): pair = lax.psum(part.astype(jnp.bfloat16), 'head')]
    all_gather x1 -> x0, blocking collectives: 13.6 us -> none  [local(): pair_weights = lax.all_gather(w_pair, 'head', axis=0, tiled=True)]
    dot_general x4 -> x0, matrix products: 8.08 us -> none  [the longest x1 3.24 us: local(): proj = jnp.dot(rows, w_proj, preferred_element_type=jnp.float32)]
    slice x7 -> x0, local copies, waits for them, and re-layouts: 5.74 us -> none  [the longest x1 1.58 us: local(): part = attention(deletions, proj[:tokens, :HD], kv, mod_all, mix)]
    ppermute x2 -> x0, starting transfers between devices: 5.33 us -> none  [the longest x1 4.04 us: local(): low = lax.ppermute(sequence[tokens - DIL:], 'ctx', forward)]
  transfers between devices with their start and end apart: 8 -> 0, of which waited for: 7 -> 0; matrix products, arithmetic and copies ran while one was open for 3% -> 0% of each run, Pallas kernels for 0% -> 0%
where the time goes in v2:
time: 123 us; the launch traced here: 122 us
  Pallas kernels  114 us (93%)
  local copies, waits for them, and re-layouts  7.54 us (6%)
    pallas_call x1, Pallas kernels, project_rows(): pl.pallas_call(rows_kernel, out_shape=(jax.ShapeDtypeStruct((tokens, HD),...  68.3 us
    pallas_call x1, Pallas kernels, attention(): pl.pallas_call(attention_kernel, out_shape=jax.ShapeDtypeStruct((variants...  20.4 us
    pallas_call x1, Pallas kernels, sum_heads(): pl.pallas_call(sum_kernel, out_shape=(jax.ShapeDtypeStruct((rows, C), jnp...  15.3 us
    pallas_call x1, Pallas kernels, pair_map(): pl.pallas_call(functools.partial(pair_kernel, per), grid=(rows // per,),...  10.1 us
    unnamed x9, local copies, waits for them, and re-layouts  7.54 us

profile of v2, /device:TPU:1, one launch (start us, length us, event | category | flops | bytes accessed | tf_op | source)
XLA Modules:
  0.0 121.7 jit_solution(11151042186274350500)
XLA Ops:
  0.0 1.3 %copy.12.dels = s32[4,2]{1,0:T(4,128)} copy(s32[4,2]{0,1:T(2,128)} %param.9) | data formatting | bytes 64 | tf_op args[1]
  1.3 1.8 %copy.10.seq = bf16[512,192]{1,0:T(8,128)(2,1)} copy(bf16[512,192]{0,1:T(8,128)(2,1)} %param.8) | data formatting | bytes 393216 | tf_op args[0]
  3.1 2.5 %copy.11.w_ref = bf16[1536,448]{1,0:T(8,128)(2,1)} copy(bf16[1536,448]{0,1:T(8,128)(2,1)} %param.12) | data formatting | bytes 2752512 | tf_op args[4]
  5.6 68.3 %shard_map.82 = (bf16[512,128]{1,0:T(8,128)(2,1)}, bf16[8,1280,128]{2,1,0:T(8,128)(2,1)}, bf16[8,672,128]{2,1,0:T(8,128)(2,1)}, bf16[4,128,192]{2,1,0:T(8,128)(2,1)}, bf16[192,256]{1,0:T(8,128)(2,1)}) custom-call(s32[4,2]{1,0:T(4,128)} %copy.12.dels, bf16[512,192]{1,0:T(8,128)(2,1)} %copy.10.seq, f32[3,192]{1,0:T(4,128)} %taps.1, f32[1,192]{1,0:T(1,128)} %bitcast.7, ...), custom_call_target="tpu_custom_call" | custom-call | tf_op jit(solution)/shard_map/pallas_call | solution.py:458
  73.9 0.0 copy-start.2
  74.0 20.4 %shard_map.83 = f32[4,128,256]{2,1,0:T(8,128)} custom-call(s32[4,2]{1,0:T(4,128)} %copy.12.dels, bf16[512,128]{1,0:T(8,128)(2,1)} %get-tuple-element.12.q_ref, bf16[8,1280,128]{2,1,0:T(8,128)(2,1)} %get-tuple-element.13.kv_ref, bf16[8,672,128]{2,1,0:T(8,128)(2,1)} %get-tuple-element.14.mod_ref, bf16[192,256]{1,0:T(8,128)(2,1)} %get-tuple-element.15.mix_ref, ...), custom_call_target="tpu_custom_call" | custom-call | tf_op jit(solution)/shard_map/pallas_call | solution.py:128
  94.3 15.3 %shard_map.84 = (f32[512,128]{1,0:T(8,128)}, f32[512,128]{1,0:T(8,128)}) custom-call(f32[512,256]{1,0:T(8,128)} %bitcast.6), custom_call_target="tpu_custom_call" | custom-call | tf_op jit(solution)/shard_map/pallas_call | solution.py:569
  109.7 0.0 copy-done.2
  109.7 0.0 copy-start
  109.7 0.9 copy-done
  110.7 0.0 copy-start.1
  110.7 0.9 copy-done.1
  111.6 10.1 %shard_map.85 = bf16[4,128,128,128]{3,2,1,0:T(8,128)(2,1)} custom-call(f32[4,128,128]{2,1,0:T(8,128)S(1)} %bitcast.4, f32[4,128,128]{2,1,0:T(8,128)S(1)} %bitcast.5, f32[16,128]{1,0:T(8,128)S(1)} %copy-done.2), custom_call_target="tpu_custom_call" | custom-call | tf_op jit(solution)/shard_map/pallas_call | solution.py:173
Async XLA Ops:
  73.9 35.8 %copy-start.2 = (f32[16,128]{1,0:T(8,128)S(1)}, f32[16,128]{1,0:T(8,128)}, u32[]{:S(2)}) copy-start(f32[16,128]{1,0:T(8,128)} %table_ref.1) | copy-start | bytes 24580
  109.7 1.0 copy-start
  110.7 0.9 copy-start.1

commit v3 on v1

v3 whole, which is shorter than its diff:
```python
import functools
import math

import jax
import jax.numpy as jnp
from jax import lax
from jax.experimental import pallas as pl
from jax.experimental.pallas import tpu as pltpu
from jax.sharding import PartitionSpec as P

HD = 128
VD = 192
C = 128
NB = 16
POOL = 4
DIL = 256
DEL = 128
SEGS = 3
BIG = -1e30
QSCALE = math.log2(math.e) / math.sqrt(HD)


def changed(delta, length):
    hit = jnp.logical_and(delta >= 0, delta < length)
    for shift in (-DIL, DIL):
        moved = delta + shift
        hit = jnp.logical_or(hit, jnp.logical_and(moved >= 0, moved < length))
    return hit


def pair_kernel(rows_per, row_ref, col_ref, table_ref, out_ref, rel, rows, cols):
    step = pl.program_id(0)
    span = col_ref.shape[1]
    row_count = row_ref.shape[1]

    @pl.when(step == 0)
    def _():
        base = lax.axis_index("head") * span - lax.axis_index("ctx") * row_count - (row_count - 1)
        dist = jnp.abs(lax.broadcasted_iota(jnp.int32, rel.shape, 0) + base)
        value = jnp.broadcast_to(table_ref[0:1, :], rel.shape)
        for k in range(NB - 1):
            value = jnp.where(dist >= 2**k, table_ref[k + 1 : k + 2, :], value)
        rel[...] = value
        rows[...] = row_ref[...].astype(jnp.float32)
        cols[...] = col_ref[...].astype(jnp.float32)

    def one(i, _):
        row = step * rows_per + i
        shifted = rel[pl.ds(row_count - 1 - row, span), :]
        for v in range(row_ref.shape[0]):
            out_ref[v, i] = (rows[v, pl.ds(row, 1), :] + (cols[v] + shifted)).astype(out_ref.dtype)
        return 0

    lax.fori_loop(0, rows_per, one, 0)


def pair_map(row_feats, col_feats, table):
    variants, rows, _ = row_feats.shape
    cols = col_feats.shape[1]
    per = 8
    vm = pl.BlockSpec(memory_space=pltpu.VMEM)
    return pl.pallas_call(
        functools.partial(pair_kernel, per),
        grid=(rows // per,),
        out_shape=jax.ShapeDtypeStruct((variants, rows, cols, C), jnp.bfloat16),
        in_specs=[vm, vm, vm],
        out_specs=pl.BlockSpec((variants, per, cols, C), lambda i: (0, i, 0, 0)),
        scratch_shapes=[
            pltpu.VMEM((rows + cols, C), jnp.float32),
            pltpu.VMEM((variants, rows, C), jnp.float32),
            pltpu.VMEM((variants, cols, C), jnp.float32),
        ],
        compiler_params=pltpu.CompilerParams(vmem_limit_bytes=32 * 2**20),
    )(row_feats, col_feats, table)


MESH = pl.DeviceIdType.MESH


def pack(x):
    half = x.shape[0] // 2
    tail = jnp.concatenate([x[:half, 128:], x[half:, 128:]], axis=1)
    return jnp.concatenate([x[:, :128], tail], axis=0)


class Ring:
    def __init__(self, make, buf, rows, base, me, dn, up, far, mate, mate_of, to_dn, to_up, to_mate):
        half = rows // 2
        self.full, self.lo, self.hi = pl.ds(0, rows), pl.ds(0, half), pl.ds(half, half)
        self.make, self.buf, self.base = make, buf, base
        self.me, self.dn, self.up, self.far, self.mate, self.mate_of = me, dn, up, far, mate, mate_of
        self.to_dn, self.to_up, self.to_mate = to_dn, to_up, to_mate
        self.sent = []

    def copy(self, slot, rows, index, target):
        ref = self.buf.at[slot, rows]
        return self.make(ref, ref, self.base + index, target)

    def send(self, slot, rows, index, target):
        made = self.copy(slot, rows, index, target)
        made.start()
        self.sent.append(made)

    def got(self, slot, rows, index):
        self.copy(slot, rows, index, self.to_up).wait_recv()


class HeadRing(Ring):
    def begin(self):
        self.send(self.me, self.full, 0, self.to_up)
        self.send(self.me, self.full, 1, self.to_dn)
        self.send(self.me, self.full, 2, self.to_mate)

    def relay(self):
        self.got(self.dn, self.full, 0)
        self.send(self.dn, self.lo, 3, self.to_up)
        self.send(self.dn, self.full, 4, self.to_mate)
        self.got(self.up, self.full, 1)
        self.send(self.up, self.hi, 5, self.to_dn)
        self.send(self.up, self.full, 6, self.to_mate)

    def end(self):
        self.got(self.far, self.lo, 3)
        self.send(self.far, self.lo, 7, self.to_mate)
        self.got(self.far, self.hi, 5)
        self.send(self.far, self.hi, 8, self.to_mate)
        self.got(self.mate, self.full, 2)
        self.got(self.mate_of(self.dn), self.full, 4)
        self.got(self.mate_of(self.up), self.full, 6)
        self.got(self.mate_of(self.far), self.lo, 7)
        self.got(self.mate_of(self.far), self.hi, 8)

    def drain(self):
        for made in self.sent:
            made.wait_send()


class TokenRing(Ring):
    def begin(self):
        self.send(self.me, self.full, 2, self.to_mate)
        self.send(self.me, self.full, 0, self.to_up)
        self.send(self.me, self.full, 1, self.to_dn)

    def cross(self):
        self.got(self.mate, self.full, 2)
        self.send(self.mate, self.full, 4, self.to_up)
        self.send(self.mate, self.full, 6, self.to_dn)

    def relay(self):
        self.got(self.dn, self.full, 0)
        self.send(self.dn, self.lo, 3, self.to_up)
        self.got(self.up, self.full, 1)
        self.send(self.up, self.hi, 5, self.to_dn)

    def relay_mate(self):
        dn, up = self.mate_of(self.dn), self.mate_of(self.up)
        self.got(dn, self.full, 4)
        self.send(dn, self.lo, 7, self.to_up)
        self.got(up, self.full, 6)
        self.send(up, self.hi, 8, self.to_dn)

    def end(self):
        self.got(self.far, self.lo, 3)
        self.got(self.far, self.hi, 5)
        self.got(self.mate_of(self.far), self.lo, 7)
        self.got(self.mate_of(self.far), self.hi, 8)

    def drain(self):
        for made in self.sent:
            made.wait_send()


def swap_lanes(x):
    return jnp.concatenate([x[:, 64:], x[:, :64]], axis=1)


def unpack_tail(tail, fill):
    both = jnp.concatenate([tail, swap_lanes(tail)], axis=0)
    keep = lax.broadcasted_iota(jnp.int32, both.shape, 1) < 64
    return jnp.where(keep, both, jnp.broadcast_to(fill, both.shape))


def features_kernel(dels, seq, taps, bias, w_ref, wo_ref, wp_ref, row_out, col_out,
                    low, high, cols, gb0, gb1, gm, wp, moved, landed, flat, kv0, kv1, mq, mkv,
                    queries, q_aug, top, acc, ka, va, pooled, mix, mine, arrived, rows_buf, cols_buf, feats,
                    send, recv):
    width, tokens = seq.shape
    variants = dels.shape[0]
    share = SEGS * DEL // 2
    per = 2 * share
    n = 8
    bf = jnp.bfloat16
    c, h, g = lax.axis_index("ctx"), lax.axis_index("head"), lax.axis_index("var")
    dn_h, up_h, far_h = lax.rem(h + 6, n), lax.rem(h + 2, n), lax.rem(h + 4, n)
    sib = h + 1 - 2 * lax.rem(h, 2)
    x0, y0 = c // 4 * 4, lax.rem(c, 4)
    up_c, dn_c, far_c = x0 + lax.rem(y0 + 1, 4), x0 + lax.rem(y0 + 3, 4), x0 + lax.rem(y0 + 2, 4)
    other = lambda t: lax.rem(t + 4, n)
    xp = other(c)
    sib_of = lambda t: t + 1 - 2 * lax.rem(t, 2)

    barrier = pltpu.get_barrier_semaphore()
    peers = [{"ctx": lax.rem(c + k, n)} for k in range(1, n)]
    peers += [{"head": lax.rem(h + k, n)} for k in range(1, n)]
    peers += [{"ctx": xp, "var": 1 - g}]
    for peer in peers:
        pl.semaphore_signal(barrier, inc=1, device_id=peer, device_id_type=MESH)
    for k in range(n):
        source = lax.rem(h + k, n)

        @pl.when(jnp.logical_or(c != h, k != 0))
        def _():
            pl.semaphore_signal(barrier, inc=1, device_id={"ctx": h, "head": source}, device_id_type=MESH)

    for k in range(4):
        line = bias[...] if k == 3 else taps[k : k + 1, :]
        cols[k] = jnp.broadcast_to(line, (128, width)).T
    wp[h] = wp_ref[...]
    pl.semaphore_wait(barrier, len(peers) + n - (c == h).astype(jnp.int32))

    def make(src, dst, index, target, arrival=None):
        return pltpu.make_async_remote_copy(
            src_ref=src, dst_ref=dst, send_sem=send.at[index],
            recv_sem=recv.at[index if arrival is None else arrival],
            device_id=target, device_id_type=MESH,
        )

    halo_low = make(seq.at[:, pl.ds(tokens - DIL, DIL)], low, 0, {"ctx": lax.rem(c + 1, n)})
    halo_high = make(seq.at[:, pl.ds(0, DIL)], high, 1, {"ctx": lax.rem(c + 7, n)})
    halo_low.start()
    halo_high.start()

    def head_ring(buf, base):
        return HeadRing(make, buf, buf.shape[1], base, h, dn_h, up_h, far_h, sib, sib_of,
                        {"head": dn_h}, {"head": up_h}, {"head": sib})

    def token_ring(buf, base, to_mate):
        return TokenRing(make, buf, buf.shape[1], base, c, dn_c, up_c, far_c, xp, other,
                         {"ctx": dn_c}, {"ctx": up_c}, to_mate)

    ring_b0, ring_b1, ring_m, ring_p = (head_ring(buf, 10 + 9 * i) for i, buf in enumerate((gb0, gb1, gm, wp)))
    cross = {"ctx": xp, "var": 1 - g}
    ring_k0, ring_k1 = token_ring(kv0, 46, cross), token_ring(kv1, 55, cross)
    ring_q, ring_o = token_ring(mq, 64, {"ctx": xp}), token_ring(mkv, 73, {"ctx": xp})

    at = lax.broadcasted_iota(jnp.int32, (1, DIL), 1) + c * tokens
    wide = lambda k: jnp.concatenate([cols[k], cols[k]], axis=1)

    def trunk(half, first, length):
        def kept(x, shift, inside=None):
            d = at + (half * DIL + shift) - first
            keep = jnp.logical_or(d < 0, d >= length)
            if inside is not None:
                keep = jnp.logical_and(keep, inside)
            return jnp.where(keep, x.astype(jnp.float32), 0.0)

        here = kept(seq[:, half * DIL : (half + 1) * DIL], 0)
        if half == 0:
            before, after = kept(low[...], -DIL, c != 0), kept(seq[:, DIL:], DIL)
        else:
            before, after = kept(seq[:, :DIL], -DIL), kept(high[...], DIL, c != n - 1)
        conv = wide(0) * before + wide(1) * here + wide(2) * after + wide(3)
        return (here + jax.nn.gelu(conv, approximate=True)).astype(bf)

    halo_low.wait()
    gb0[h] = trunk(0, 0, 0)
    ring_b0.begin()
    halo_high.wait()
    gb1[h] = trunk(1, 0, 0)
    ring_b1.begin()

    r = lax.broadcasted_iota(jnp.int32, (tokens, share), 1)
    offset = (r // (DEL // 2) - 1) * DIL + r % (DEL // 2)
    here = lax.broadcasted_iota(jnp.int32, (tokens, share), 0) + c * tokens - offset
    pool = (
        lax.broadcasted_iota(jnp.int32, (tokens // POOL, tokens), 1) // POOL
        == lax.broadcasted_iota(jnp.int32, (tokens // POOL, tokens), 0)
    ).astype(bf)

    def variant(v, _):
        first = dels[v, 0]
        length = dels[v, 1] - first
        own = jnp.concatenate([trunk(0, first, length), trunk(1, first, length)], axis=1)
        for half in range(2):
            pick = (here == first + half * (DEL // 2)).astype(bf)
            moved[2 * v + half] = pack(jnp.dot(own, pick, preferred_element_type=jnp.float32).astype(bf))
        mean = lax.dot_general(pool, own, (((1,), (1,)), ((), ())), preferred_element_type=jnp.float32)
        pooled[v] = (mean * (1.0 / POOL)).astype(bf)
        return 0

    lax.fori_loop(0, variants, variant, 0)
    shared = []
    for k in range(1, n):
        to = lax.rem(c + k, n)
        made = make(moved.at[to], landed.at[k - 1], 1 + k, {"ctx": to})
        made.start()
        shared.append(made)
    ring_b0.relay()
    total = moved[c]
    for k in range(1, n):
        shared[k - 1].wait_recv()
        total = total + landed[k - 1]
    gm[h] = total
    ring_m.begin()
    ring_b0.end()

    def project(x):
        return jnp.dot(w_ref[...], x, preferred_element_type=jnp.float32).T

    def place(kv, x, count):
        kv[c, :count] = x[:count, HD : 2 * HD].astype(bf)
        kv[c, count:] = pack(x[:count, 2 * HD :].astype(bf))

    x = project(gb0[...].reshape(n * width, DIL))
    place(kv0, x, DIL)
    ring_k0.begin()
    queries[:DIL] = (x[:, :HD] * QSCALE).astype(bf)
    ring_m.relay()
    ring_b1.relay()
    ring_p.begin()
    ring_m.end()
    zero = jnp.zeros((1, 128), bf)
    for k in range(n):
        flat[k * width : (k + 1) * width, :128] = gm[k, :width]
        flat[k * width : (k + 1) * width, 128:] = unpack_tail(gm[k, width:], zero)
    x = project(flat[...])
    mq[c] = (x[:share, :HD] * QSCALE).astype(bf)
    ring_q.begin()
    place(mkv, x, share)
    ring_b1.end()
    x = project(gb1[...].reshape(n * width, DIL))
    place(kv1, x, DIL)
    ring_k1.begin()
    ring_o.begin()
    queries[DIL:] = (x[:, :HD] * QSCALE).astype(bf)
    ring_k0.cross()
    ring_k0.relay()
    ring_q.cross()
    ring_q.relay()
    ring_p.relay()
    ring_p.end()
    total = jnp.zeros((wo_ref.shape[0], 2 * C), jnp.float32)
    for k in range(0, n, 2):
        two = jnp.concatenate([wp[k], wp[k + 1]], axis=0)
        total = total + jnp.dot(wo_ref[:, k * width : (k + 2) * width], two, preferred_element_type=jnp.float32)
    mix[...] = total.astype(bf)
    ring_q.relay_mate()
    ring_q.end()

    lane = lax.broadcasted_iota(jnp.int32, (1, 128), 1)
    first = jnp.zeros((1, 128), jnp.int32)
    length = jnp.zeros((1, 128), jnp.int32)
    for v in range(variants):
        first = jnp.where(lane == v, dels[v, 0], first)
        length = jnp.where(lane == v, dels[v, 1] - dels[v, 0], length)
    col = lax.broadcasted_iota(jnp.int32, (tokens, per), 1)
    col_step = col // share * (DEL // 2) + col % (DEL // 2)
    col_offset = (col % share // (DEL // 2) - 1) * DIL + col_step
    qpos = lax.broadcasted_iota(jnp.int32, (tokens, per), 0) + c * tokens

    def aim(v, _):
        s0 = dels[v, 0]
        count = dels[v, 1] - s0
        spot = jnp.logical_and(qpos - col_offset == s0, col_step < count).astype(bf)
        source = jnp.concatenate([mq[2 * v], mq[2 * v + 1]], axis=0)
        moved_q = jnp.dot(spot, source, preferred_element_type=jnp.float32)
        is_mod = changed(qpos[:, :128] - s0, count)
        q_aug[v, :, :HD] = jnp.where(is_mod, moved_q, queries[...].astype(jnp.float32)).astype(bf)
        q_aug[v, :, HD:] = jnp.broadcast_to(jnp.where(lane == v, 1.0, 0.0), (tokens, 128)).astype(bf)
        top[v] = jnp.full((tokens, 1), -3e38, jnp.float32)
        acc[v] = jnp.zeros((tokens, 256), jnp.float32)
        return 0

    lax.fori_loop(0, variants, aim, 0)
    ones = jnp.where(lane == VD - 128, 1.0, 0.0).astype(bf)

    def unit(v, keys, values):
        s = lax.dot_general(q_aug[v], keys, (((1,), (1,)), ((), ())), preferred_element_type=jnp.float32)
        old = top[v]
        new = jnp.maximum(old, s.max(1, keepdims=True))
        w = jnp.exp2(s - new).astype(bf)
        top[v] = new
        acc[v] = acc[v] * jnp.exp2(old - new) + jnp.dot(w, values, preferred_element_type=jnp.float32)

    def attend(block):
        for i, kv in enumerate((kv0, kv1)):
            rows = slice(i * DIL, (i + 1) * DIL)
            ka[rows, :HD] = kv[block, :DIL]
            pos = lax.broadcasted_iota(jnp.int32, (DIL, 128), 0) + (block * tokens + i * DIL)
            ka[rows, HD:] = jnp.where(changed(pos - first, length), BIG, 0.0).astype(bf)
            va[rows, :128] = kv[block, DIL : 2 * DIL]
            va[rows, 128:] = unpack_tail(kv[block, 2 * DIL :], ones)

        def one(v, _):
            unit(v, ka[...], va[...])
            return 0

        lax.fori_loop(0, variants, one, 0)

    ring_k1.cross()
    ring_k1.relay()
    attend(c)
    ring_k0.relay_mate()
    ring_o.cross()
    ring_o.relay()
    attend(dn_c)
    ring_k1.relay_mate()
    attend(up_c)
    ring_o.relay_mate()
    attend(xp)
    ring_k0.end()
    ring_k1.end()
    attend(far_c)
    attend(other(dn_c))
    attend(other(up_c))
    attend(other(far_c))
    ring_o.end()

    row = lax.broadcasted_iota(jnp.int32, (per, 128), 0)
    step = row // share * (DEL // 2) + row % (DEL // 2)
    row_offset = (row % share // (DEL // 2) - 1) * DIL + step
    count = tokens // POOL // 2
    first_sent = []
    for v in range(variants):
        token = dels[v, 0] + row_offset
        valid = (step < dels[v, 1] - dels[v, 0]) & (token >= 0) & (token < n * tokens)
        ka[:per, HD:] = jnp.where(valid, 0.0, BIG).astype(bf)
        for i in range(2):
            rows = slice(i * share, (i + 1) * share)
            ka[rows, :HD] = mkv[2 * v + i, :share]
            va[rows, :128] = mkv[2 * v + i, share : 2 * share]
            va[rows, 128:] = unpack_tail(mkv[2 * v + i, 2 * share :], ones)
        unit(v, ka[:per], va[:per])
        out = (acc[v, :, :VD] / acc[v, :, VD : VD + 1]).astype(bf)
        mean = jnp.dot(pool, out, preferred_element_type=jnp.float32) * (1.0 / POOL)
        part = jnp.dot(mean.astype(bf), mix[...], preferred_element_type=jnp.float32) + jnp.dot(
            pooled[v], wp_ref[...], preferred_element_type=jnp.float32
        )
        for i in range(2):
            to = 2 * v + i
            mine[to] = part[i * count : (i + 1) * count].astype(bf)
            made = make(mine.at[to], arrived.at[h], 82 + to, {"head": to}, 82 + h)
            first_sent.append(made)

            @pl.when(h != to)
            def _():
                made.start()

            @pl.when(h == to)
            def _():
                arrived[h] = mine[to]

    for k in range(n):
        @pl.when(h != k)
        def _():
            make(mine.at[k], arrived.at[k], 82 + k, {"head": k}).wait_recv()

    total = arrived[0].astype(jnp.float32)
    for k in range(1, n):
        total = total + arrived[k].astype(jnp.float32)
    feats[0] = total[:, :C].astype(bf)
    feats[1] = total[:, C:].astype(bf)
    rows_buf[h] = feats[0]
    for k in range(n):
        to = lax.rem(c + k, n)

        @pl.when(jnp.logical_or(c != h, k != 0))
        def _():
            make(feats.at[1], cols_buf.at[h], 98 + k, {"ctx": to, "head": c}, 98 + h).start()

        @pl.when(jnp.logical_and(c == h, k == 0))
        def _():
            cols_buf[h] = feats[1]

    for k in range(1, n):
        make(feats.at[0], rows_buf.at[h], 90 + k, {"head": lax.rem(h + k, n)}).start()
    for ring in (ring_b0, ring_b1, ring_m, ring_p, ring_k0, ring_k1, ring_q, ring_o):
        ring.drain()
    for made in shared:
        made.wait_send()
    for k, made in enumerate(first_sent):
        @pl.when(h != k)
        def _():
            made.wait_send()

    for k in range(1, n):
        source = lax.rem(h + n - k, n)
        made = make(feats.at[0], rows_buf.at[source], 90 + k, {"head": lax.rem(h + k, n)})
        made.wait_recv()
        made.wait_send()
    for k in range(n):
        @pl.when(jnp.logical_or(c != h, k != h))
        def _():
            make(feats.at[1], cols_buf.at[k], 98 + k, {"head": lax.rem(h + 1, n)}).wait_recv()

        @pl.when(jnp.logical_or(c != h, k != 0))
        def _():
            make(feats.at[1], cols_buf.at[h], 98 + k, {"head": lax.rem(h + 1, n)}).wait_send()
    row_out[...] = rows_buf[...]
    col_out[...] = cols_buf[...]


def features(sequence, deletions, conv_taps, conv_bias, w_proj, w_out, w_pair):
    tokens, width = sequence.shape
    variants = deletions.shape[0]
    n = 8
    share = SEGS * DEL // 2
    vm = pl.BlockSpec(memory_space=pltpu.VMEM)
    bf, f32 = jnp.bfloat16, jnp.float32
    part = variants * tokens // POOL // n
    scratch = [
        ((width, DIL), bf),
        ((width, DIL), bf),
        ((4, width, 128), f32),
        ((n, width, DIL), bf),
        ((n, width, DIL), bf),
        ((n, share * 3 // 2, 128), bf),
        ((n, width, 2 * C), bf),
        ((n, share * 3 // 2, 128), bf),
        ((n - 1, share * 3 // 2, 128), bf),
        ((n * width, 256), bf),
        ((n, DIL * 5 // 2, 128), bf),
        ((n, DIL * 5 // 2, 128), bf),
        ((n, share, 128), bf),
        ((n, share * 5 // 2, 128), bf),
        ((tokens, HD), bf),
        ((variants, tokens, 256), bf),
        ((variants, tokens, 1), f32),
        ((variants, tokens, 256), f32),
        ((tokens, 256), bf),
        ((tokens, 256), bf),
        ((variants, tokens // POOL, width), bf),
        ((w_out.shape[0], 2 * C), bf),
        ((n, part, 2 * C), bf),
        ((n, part, 2 * C), bf),
        ((n, part, C), bf),
        ((n, part, C), bf),
        ((2, part, C), bf),
    ]
    return pl.pallas_call(
        features_kernel,
        out_shape=(jax.ShapeDtypeStruct((n, part, C), bf),) * 2,
        in_specs=[pl.BlockSpec(memory_space=pltpu.SMEM)] + [vm] * 6,
        out_specs=(vm, vm),
        scratch_shapes=[pltpu.VMEM(shape, kind) for shape, kind in scratch]
        + [pltpu.SemaphoreType.DMA((106,)), pltpu.SemaphoreType.DMA((106,))],
        compiler_params=pltpu.CompilerParams(
            collective_id=0, has_side_effects=True, vmem_limit_bytes=56 * 2**20
        ),
    )(deletions, sequence.T, conv_taps, conv_bias.reshape(1, width), w_proj.T, w_out, w_pair)


def local(sequence, deletions, conv_taps, conv_bias, w_proj, w_out, w_pair, dist_table):
    variants = deletions.shape[0]
    row_feats, col_feats = features(sequence, deletions, conv_taps, conv_bias, w_proj, w_out, w_pair)
    shape = (variants, sequence.shape[0] // POOL, C)
    return pair_map(row_feats.reshape(shape), col_feats.reshape(shape), dist_table)


def solution(mesh):
    in_specs = (
        P("ctx", "head"),
        P("var", None),
        P(None, "head"),
        P("head"),
        P(None, "head"),
        P("head", None),
        P("head", None),
        P(),
    )
    out_specs = P("var", "ctx", "head", None)
    return jax.shard_map(local, mesh=mesh, in_specs=in_specs, out_specs=out_specs, check_vma=False)
```

time: 391 us -> 132 us (0.34)
  waiting for transfers between devices: 295 us -> 0 us
  Pallas kernels: 30.6 us -> 127 us
  between operations: 13.7 us -> 0.02 us
  blocking collectives: 13.6 us -> 0 us
  other arithmetic: 9.69 us -> 0 us
  local copies, waits for them, and re-layouts: 12.8 us -> 3.83 us
  matrix products: 8.08 us -> 0 us
  starting transfers between devices: 5.54 us -> 0 us
    all_gather x4 -> x0, waiting for transfers between devices: 162 us -> none  [the longest x1 63.8 us: local(): kv = lax.all_gather(proj[:tokens, HD:], 'ctx', axis=0, tiled=True)]
    pallas_call x1, Pallas kernels: 20.5 us -> 117 us  [features(): pl.pallas_call(features_kernel, out_shape=(jax.ShapeDtypeStruct((n, part,...]
    unnamed x7 -> x0, waiting for transfers between devices: 75.5 us -> none
    psum x1 -> x0, waiting for transfers between devices: 56.4 us -> none  [local(): pair = lax.psum(part.astype(jnp.bfloat16), 'head')]
    all_gather x1 -> x0, blocking collectives: 13.6 us -> none  [local(): pair_weights = lax.all_gather(w_pair, 'head', axis=0, tiled=True)]
    dot_general x4 -> x0, matrix products: 8.08 us -> none  [the longest x1 3.24 us: local(): proj = jnp.dot(rows, w_proj, preferred_element_type=jnp.float32)]
    slice x7 -> x0, local copies, waits for them, and re-layouts: 5.74 us -> none  [the longest x1 1.58 us: local(): part = attention(deletions, proj[:tokens, :HD], kv, mod_all, mix)]
    ppermute x2 -> x0, starting transfers between devices: 5.33 us -> none  [the longest x1 4.04 us: local(): low = lax.ppermute(sequence[tokens - DIL:], 'ctx', forward)]
  transfers between devices with their start and end apart: 8 -> 0, of which waited for: 7 -> 0; matrix products, arithmetic and copies ran while one was open for 3% -> 0% of each run, Pallas kernels for 0% -> 0%
where the time goes in v3:
time: 132 us; the launch traced here: 131 us
  Pallas kernels  127 us (96%)
  local copies, waits for them, and re-layouts  3.83 us (3%)
    pallas_call x1, Pallas kernels, features(): pl.pallas_call(features_kernel, out_shape=(jax.ShapeDtypeStruct((n, part,...  117 us
    pallas_call x1, Pallas kernels, pair_map(): pl.pallas_call(functools.partial(pair_kernel, per), grid=(rows // per,),...  10.1 us
    unnamed x7, local copies, waits for them, and re-layouts  3.83 us

profile of v3, /device:TPU:1, one launch (start us, length us, event | category | flops | bytes accessed | tf_op | source)
XLA Modules:
  0.0 130.9 jit_solution(2613084548085010708)
XLA Ops:
  0.0 1.3 %copy.9.dels = s32[4,2]{1,0:T(4,128)} copy(s32[4,2]{0,1:T(2,128)} %param.9) | data formatting | bytes 64 | tf_op args[1]
  1.3 117.0 %shard_map.82 = (bf16[8,64,128]{2,1,0:T(8,128)(2,1)}, bf16[8,64,128]{2,1,0:T(8,128)(2,1)}) custom-call(s32[4,2]{1,0:T(4,128)} %copy.9.dels, bf16[192,512]{1,0:T(8,128)(2,1)} %bitcast.8, f32[3,192]{1,0:T(4,128)} %taps.1, f32[1,192]{1,0:T(1,128)} %bitcast.9, bf16[448,1536]{1,0:T(8,128)(2,1)} %bitcast.7, bf16[192,1536]{1,0:T(8,128)(2,1)} %wo_ref.1, ...), custom_call_target="tpu_custom_call" | custom-call | tf_op jit(solution)/shard_map/pallas_call | solution.py:540
  118.3 0.0 copy-start
  118.3 0.9 copy-done
  119.2 0.0 copy-start.1
  119.2 0.9 copy-done.1
  120.1 0.0 copy-start.2
  120.1 0.7 copy-done.2
  120.8 10.1 %shard_map.83 = bf16[4,128,128,128]{3,2,1,0:T(8,128)(2,1)} custom-call(bf16[4,128,128]{2,1,0:T(8,128)(2,1)S(1)} %bitcast.5, bf16[4,128,128]{2,1,0:T(8,128)(2,1)S(1)} %bitcast.6, f32[16,128]{1,0:T(8,128)S(1)} %copy-done.2), custom_call_target="tpu_custom_call" | custom-call | tf_op jit(solution)/shard_map/pallas_call | solution.py:62
Async XLA Ops:
  118.3 0.9 copy-start
  119.2 0.9 copy-start.1
  120.1 0.7 copy-start.2

commit v4 on v3

--- a/solution.py
+++ b/solution.py
@@ -152,16 +152,15 @@
         self.got(self.up, self.full, 1)
         self.send(self.up, self.hi, 5, self.to_dn)
 
-    def relay_mate(self):
-        dn, up = self.mate_of(self.dn), self.mate_of(self.up)
-        self.got(dn, self.full, 4)
-        self.send(dn, self.lo, 7, self.to_up)
-        self.got(up, self.full, 6)
-        self.send(up, self.hi, 8, self.to_dn)
+    def far_block(self):
+        self.got(self.far, self.lo, 3)
+        self.send(self.far, self.lo, 7, self.to_mate)
+        self.got(self.far, self.hi, 5)
+        self.send(self.far, self.hi, 8, self.to_mate)
 
     def end(self):
-        self.got(self.far, self.lo, 3)
-        self.got(self.far, self.hi, 5)
+        self.got(self.mate_of(self.dn), self.full, 4)
+        self.got(self.mate_of(self.up), self.full, 6)
         self.got(self.mate_of(self.far), self.lo, 7)
         self.got(self.mate_of(self.far), self.hi, 8)
 
@@ -222,7 +221,7 @@
         return pltpu.make_async_remote_copy(
             src_ref=src, dst_ref=dst, send_sem=send.at[index],
             recv_sem=recv.at[index if arrival is None else arrival],
-            device_id=target, device_id_type=MESH,
+            device_id=(target.get("ctx", c), target.get("head", h), target.get("var", g)), device_id_type=MESH,
         )
 
     halo_low = make(seq.at[:, pl.ds(tokens - DIL, DIL)], low, 0, {"ctx": lax.rem(c + 1, n)})
@@ -262,6 +261,7 @@
         conv = wide(0) * before + wide(1) * here + wide(2) * after + wide(3)
         return (here + jax.nn.gelu(conv, approximate=True)).astype(bf)
 
+    ring_p.begin()
     halo_low.wait()
     gb0[h] = trunk(0, 0, 0)
     ring_b0.begin()
@@ -288,6 +288,7 @@
         pooled[v] = (mean * (1.0 / POOL)).astype(bf)
         return 0
 
+    ring_p.relay()
     lax.fori_loop(0, variants, variant, 0)
     shared = []
     for k in range(1, n):
@@ -317,7 +318,7 @@
     queries[:DIL] = (x[:, :HD] * QSCALE).astype(bf)
     ring_m.relay()
     ring_b1.relay()
-    ring_p.begin()
+    ring_p.end()
     ring_m.end()
     zero = jnp.zeros((1, 128), bf)
     for k in range(n):
@@ -337,14 +338,12 @@
     ring_k0.relay()
     ring_q.cross()
     ring_q.relay()
-    ring_p.relay()
-    ring_p.end()
     total = jnp.zeros((wo_ref.shape[0], 2 * C), jnp.float32)
     for k in range(0, n, 2):
         two = jnp.concatenate([wp[k], wp[k + 1]], axis=0)
         total = total + jnp.dot(wo_ref[:, k * width : (k + 2) * width], two, preferred_element_type=jnp.float32)
     mix[...] = total.astype(bf)
-    ring_q.relay_mate()
+    ring_q.far_block()
     ring_q.end()
 
     lane = lax.broadcasted_iota(jnp.int32, (1, 128), 1)
@@ -367,7 +366,7 @@
         is_mod = changed(qpos[:, :128] - s0, count)
         q_aug[v, :, :HD] = jnp.where(is_mod, moved_q, queries[...].astype(jnp.float32)).astype(bf)
         q_aug[v, :, HD:] = jnp.broadcast_to(jnp.where(lane == v, 1.0, 0.0), (tokens, 128)).astype(bf)
-        top[v] = jnp.full((tokens, 1), -3e38, jnp.float32)
+        top[v] = jnp.full((tokens, 128), -3e38, jnp.float32)
         acc[v] = jnp.zeros((tokens, 256), jnp.float32)
         return 0
 
@@ -377,12 +376,23 @@
     def unit(v, keys, values):
         s = lax.dot_general(q_aug[v], keys, (((1,), (1,)), ((), ())), preferred_element_type=jnp.float32)
         old = top[v]
-        new = jnp.maximum(old, s.max(1, keepdims=True))
-        w = jnp.exp2(s - new).astype(bf)
+        new = jnp.maximum(old, jnp.broadcast_to(s.max(1, keepdims=True), old.shape))
+        w = jnp.exp2(s - jnp.concatenate([new] * (keys.shape[0] // 128), axis=1)).astype(bf)
+        shrink = jnp.exp2(old - new)
         top[v] = new
-        acc[v] = acc[v] * jnp.exp2(old - new) + jnp.dot(w, values, preferred_element_type=jnp.float32)
-
-    def attend(block):
+        acc[v] = acc[v] * jnp.concatenate([shrink, shrink], axis=1) + jnp.dot(
+            w, values, preferred_element_type=jnp.float32
+        )
+
+    ring_k1.cross()
+    ring_k1.relay()
+
+    def attend(step, _):
+        look = lambda table: sum((step == i).astype(jnp.int32) * t for i, t in enumerate(table) if t)
+        away = look((0, 3, 1, 0, 2, 3, 1, 2))
+        across = look((0, 0, 0, 1, 0, 1, 1, 1))
+        side = x0 + across * (4 - 2 * x0)
+        block = side + lax.rem(y0 + away, 4)
         for i, kv in enumerate((kv0, kv1)):
             rows = slice(i * DIL, (i + 1) * DIL)
             ka[rows, :HD] = kv[block, :DIL]
@@ -390,30 +400,20 @@
             ka[rows, HD:] = jnp.where(changed(pos - first, length), BIG, 0.0).astype(bf)
             va[rows, :128] = kv[block, DIL : 2 * DIL]
             va[rows, 128:] = unpack_tail(kv[block, 2 * DIL :], ones)
-
-        def one(v, _):
+        for v in range(variants):
             unit(v, ka[...], va[...])
-            return 0
-
-        lax.fori_loop(0, variants, one, 0)
-
-    ring_k1.cross()
-    ring_k1.relay()
-    attend(c)
-    ring_k0.relay_mate()
+        return 0
+
+    lax.fori_loop(0, 2, attend, 0)
+    ring_k0.far_block()
+    ring_k1.far_block()
     ring_o.cross()
     ring_o.relay()
-    attend(dn_c)
-    ring_k1.relay_mate()
-    attend(up_c)
-    ring_o.relay_mate()
-    attend(xp)
+    lax.fori_loop(2, 5, attend, 0)
     ring_k0.end()
     ring_k1.end()
-    attend(far_c)
-    attend(other(dn_c))
-    attend(other(up_c))
-    attend(other(far_c))
+    ring_o.far_block()
+    lax.fori_loop(5, n, attend, 0)
     ring_o.end()
 
     row = lax.broadcasted_iota(jnp.int32, (per, 128), 0)
@@ -525,7 +525,7 @@
         ((n, share * 5 // 2, 128), bf),
         ((tokens, HD), bf),
         ((variants, tokens, 256), bf),
-        ((variants, tokens, 1), f32),
+        ((variants, tokens, 128), f32),
         ((variants, tokens, 256), f32),
         ((tokens, 256), bf),
         ((tokens, 256), bf),

time: 132 us -> 108 us (0.82)
  Pallas kernels: 127 us -> 104 us
    pallas_call x1, Pallas kernels: 117 us -> 93.9 us  [features(): pl.pallas_call(features_kernel, out_shape=(jax.ShapeDtypeStruct((n, part,...]
where the time goes in v4:
time: 108 us
  Pallas kernels  104 us (96%)
  local copies, waits for them, and re-layouts  3.83 us (4%)
    pallas_call x1, Pallas kernels, features(): pl.pallas_call(features_kernel, out_shape=(jax.ShapeDtypeStruct((n, part,...  93.9 us
    pallas_call x1, Pallas kernels, pair_map(): pl.pallas_call(functools.partial(pair_kernel, per), grid=(rows // per,),...  10.1 us
    unnamed x7, local copies, waits for them, and re-layouts  3.83 us

profile of v4, /device:TPU:1, one launch (start us, length us, event | category | flops | bytes accessed | tf_op | source)
XLA Modules:
  0.0 107.9 jit_solution(13764774101481245897)
XLA Ops:
  0.0 1.3 %copy.9.dels = s32[4,2]{1,0:T(4,128)} copy(s32[4,2]{0,1:T(2,128)} %param.9) | data formatting | bytes 64 | tf_op args[1]
  1.3 93.9 %shard_map.82 = (bf16[8,64,128]{2,1,0:T(8,128)(2,1)}, bf16[8,64,128]{2,1,0:T(8,128)(2,1)}) custom-call(s32[4,2]{1,0:T(4,128)} %copy.9.dels, bf16[192,512]{1,0:T(8,128)(2,1)} %bitcast.8, f32[3,192]{1,0:T(4,128)} %taps.1, f32[1,192]{1,0:T(1,128)} %bitcast.9, bf16[448,1536]{1,0:T(8,128)(2,1)} %bitcast.7, bf16[192,1536]{1,0:T(8,128)(2,1)} %wo_ref.1, ...), custom_call_target="tpu_custom_call" | custom-call | tf_op jit(solution)/shard_map/pallas_call | solution.py:540
  95.2 0.0 copy-start
  95.3 0.9 copy-done
  96.2 0.0 copy-start.1
  96.2 0.9 copy-done.1
  97.1 0.0 copy-start.2
  97.1 0.7 copy-done.2
  97.8 10.1 %shard_map.83 = bf16[4,128,128,128]{3,2,1,0:T(8,128)(2,1)} custom-call(bf16[4,128,128]{2,1,0:T(8,128)(2,1)S(1)} %bitcast.5, bf16[4,128,128]{2,1,0:T(8,128)(2,1)S(1)} %bitcast.6, f32[16,128]{1,0:T(8,128)S(1)} %copy-done.2), custom_call_target="tpu_custom_call" | custom-call | tf_op jit(solution)/shard_map/pallas_call | solution.py:62
Async XLA Ops:
  95.2 0.9 copy-start
  96.2 0.9 copy-start.1
  97.1 0.7 copy-start.2

commit v5 on v4

--- a/solution.py
+++ b/solution.py
@@ -70,7 +70,7 @@
             pltpu.VMEM((variants, rows, C), jnp.float32),
             pltpu.VMEM((variants, cols, C), jnp.float32),
         ],
-        compiler_params=pltpu.CompilerParams(vmem_limit_bytes=32 * 2**20),
+        compiler_params=pltpu.CompilerParams(vmem_limit_bytes=60 * 2**20),
     )(row_feats, col_feats, table)
 
 
@@ -184,7 +184,7 @@
                     queries, q_aug, top, acc, ka, va, pooled, mix, mine, arrived, rows_buf, cols_buf, feats,
                     send, recv):
     width, tokens = seq.shape
-    variants = dels.shape[0]
+    variants = dels.shape[1]
     share = SEGS * DEL // 2
     per = 2 * share
     n = 8
@@ -215,6 +215,18 @@
         line = bias[...] if k == 3 else taps[k : k + 1, :]
         cols[k] = jnp.broadcast_to(line, (128, width)).T
     wp[h] = wp_ref[...]
+    run = DEL // 2
+    r = lax.broadcasted_iota(jnp.int32, (tokens, 4 * run), 1)
+    offset = (r // run - 2) * DIL + (r // (2 * run)) * DIL + r % run
+    local_token = lax.broadcasted_iota(jnp.int32, (tokens, 4 * run), 0) + c * tokens - offset
+
+    def gather_runs(v, _):
+        for half in range(2):
+            pick = (local_token == dels[0, v] + half * run).astype(bf)
+            moved[2 * v + half] = jnp.dot(seq[...], pick, preferred_element_type=jnp.float32).astype(bf)
+        return 0
+
+    lax.fori_loop(0, variants, gather_runs, 0)
     pl.semaphore_wait(barrier, len(peers) + n - (c == h).astype(jnp.int32))
 
     def make(src, dst, index, target, arrival=None):
@@ -228,6 +240,12 @@
     halo_high = make(seq.at[:, pl.ds(0, DIL)], high, 1, {"ctx": lax.rem(c + 7, n)})
     halo_low.start()
     halo_high.start()
+    shared = []
+    for k in (4, 3, 5, 2, 6, 1, 7):
+        to = lax.rem(c + k, n)
+        made = make(moved.at[to], landed.at[k - 1], 1 + k, {"ctx": to})
+        made.start()
+        shared.append(made)
 
     def head_ring(buf, base):
         return HeadRing(make, buf, buf.shape[1], base, h, dn_h, up_h, far_h, sib, sib_of,
@@ -269,42 +287,11 @@
     gb1[h] = trunk(1, 0, 0)
     ring_b1.begin()
 
-    r = lax.broadcasted_iota(jnp.int32, (tokens, share), 1)
-    offset = (r // (DEL // 2) - 1) * DIL + r % (DEL // 2)
-    here = lax.broadcasted_iota(jnp.int32, (tokens, share), 0) + c * tokens - offset
     pool = (
         lax.broadcasted_iota(jnp.int32, (tokens // POOL, tokens), 1) // POOL
         == lax.broadcasted_iota(jnp.int32, (tokens // POOL, tokens), 0)
     ).astype(bf)
 
-    def variant(v, _):
-        first = dels[v, 0]
-        length = dels[v, 1] - first
-        own = jnp.concatenate([trunk(0, first, length), trunk(1, first, length)], axis=1)
-        for half in range(2):
-            pick = (here == first + half * (DEL // 2)).astype(bf)
-            moved[2 * v + half] = pack(jnp.dot(own, pick, preferred_element_type=jnp.float32).astype(bf))
-        mean = lax.dot_general(pool, own, (((1,), (1,)), ((), ())), preferred_element_type=jnp.float32)
-        pooled[v] = (mean * (1.0 / POOL)).astype(bf)
-        return 0
-
-    ring_p.relay()
-    lax.fori_loop(0, variants, variant, 0)
-    shared = []
-    for k in range(1, n):
-        to = lax.rem(c + k, n)
-        made = make(moved.at[to], landed.at[k - 1], 1 + k, {"ctx": to})
-        made.start()
-        shared.append(made)
-    ring_b0.relay()
-    total = moved[c]
-    for k in range(1, n):
-        shared[k - 1].wait_recv()
-        total = total + landed[k - 1]
-    gm[h] = total
-    ring_m.begin()
-    ring_b0.end()
-
     def project(x):
         return jnp.dot(w_ref[...], x, preferred_element_type=jnp.float32).T
 
@@ -312,12 +299,37 @@
         kv[c, :count] = x[:count, HD : 2 * HD].astype(bf)
         kv[c, count:] = pack(x[:count, 2 * HD :].astype(bf))
 
+    ring_b0.relay()
+    ring_p.relay()
+    ring_b0.end()
     x = project(gb0[...].reshape(n * width, DIL))
     place(kv0, x, DIL)
     ring_k0.begin()
     queries[:DIL] = (x[:, :HD] * QSCALE).astype(bf)
+    ring_b1.relay()
+
+    total = moved[c].astype(jnp.float32)
+    for made in shared:
+        made.wait_recv()
+    for k in range(1, n):
+        total = total + landed[k - 1].astype(jnp.float32)
+    runs = [total[:, i * run : (i + 1) * run] for i in range(4)]
+    nil = jnp.zeros((width, run), jnp.float32)
+    t0, t1, t2, t3 = (cols[k, :, :run] for k in range(4))
+    made_rows = []
+    for before, here, after in ((runs[0], runs[1], nil), (runs[1], nil, runs[2]), (nil, runs[2], runs[3])):
+        conv = t0 * before + t1 * here + t2 * after + t3
+        made_rows.append((here + jax.nn.gelu(conv, approximate=True)).astype(bf))
+    tail = made_rows[2]
+    gm[h, :width] = jnp.concatenate(made_rows[:2], axis=1)
+    gm[h, width:] = jnp.concatenate([tail[: width // 2], tail[width // 2 :]], axis=1)
+    ring_m.begin()
+    ring_b1.end()
+    x = project(gb1[...].reshape(n * width, DIL))
+    place(kv1, x, DIL)
+    ring_k1.begin()
+    queries[DIL:] = (x[:, :HD] * QSCALE).astype(bf)
     ring_m.relay()
-    ring_b1.relay()
     ring_p.end()
     ring_m.end()
     zero = jnp.zeros((1, 128), bf)
@@ -328,14 +340,21 @@
     mq[c] = (x[:share, :HD] * QSCALE).astype(bf)
     ring_q.begin()
     place(mkv, x, share)
-    ring_b1.end()
-    x = project(gb1[...].reshape(n * width, DIL))
-    place(kv1, x, DIL)
-    ring_k1.begin()
     ring_o.begin()
-    queries[DIL:] = (x[:, :HD] * QSCALE).astype(bf)
     ring_k0.cross()
     ring_k0.relay()
+
+    def variant(v, _):
+        first = dels[0, v]
+        length = dels[1, v] - first
+        own = jnp.concatenate([trunk(0, first, length), trunk(1, first, length)], axis=1)
+        mean = lax.dot_general(pool, own, (((1,), (1,)), ((), ())), preferred_element_type=jnp.float32)
+        pooled[v] = (mean * (1.0 / POOL)).astype(bf)
+        return 0
+
+    lax.fori_loop(0, variants, variant, 0)
+    ring_k1.cross()
+    ring_k1.relay()
     ring_q.cross()
     ring_q.relay()
     total = jnp.zeros((wo_ref.shape[0], 2 * C), jnp.float32)
@@ -350,16 +369,16 @@
     first = jnp.zeros((1, 128), jnp.int32)
     length = jnp.zeros((1, 128), jnp.int32)
     for v in range(variants):
-        first = jnp.where(lane == v, dels[v, 0], first)
-        length = jnp.where(lane == v, dels[v, 1] - dels[v, 0], length)
+        first = jnp.where(lane == v, dels[0, v], first)
+        length = jnp.where(lane == v, dels[1, v] - dels[0, v], length)
     col = lax.broadcasted_iota(jnp.int32, (tokens, per), 1)
     col_step = col // share * (DEL // 2) + col % (DEL // 2)
     col_offset = (col % share // (DEL // 2) - 1) * DIL + col_step
     qpos = lax.broadcasted_iota(jnp.int32, (tokens, per), 0) + c * tokens
 
     def aim(v, _):
-        s0 = dels[v, 0]
-        count = dels[v, 1] - s0
+        s0 = dels[0, v]
+        count = dels[1, v] - s0
         spot = jnp.logical_and(qpos - col_offset == s0, col_step < count).astype(bf)
         source = jnp.concatenate([mq[2 * v], mq[2 * v + 1]], axis=0)
         moved_q = jnp.dot(spot, source, preferred_element_type=jnp.float32)
@@ -383,9 +402,6 @@
         acc[v] = acc[v] * jnp.concatenate([shrink, shrink], axis=1) + jnp.dot(
             w, values, preferred_element_type=jnp.float32
         )
-
-    ring_k1.cross()
-    ring_k1.relay()
 
     def attend(step, _):
         look = lambda table: sum((step == i).astype(jnp.int32) * t for i, t in enumerate(table) if t)
@@ -422,8 +438,8 @@
     count = tokens // POOL // 2
     first_sent = []
     for v in range(variants):
-        token = dels[v, 0] + row_offset
-        valid = (step < dels[v, 1] - dels[v, 0]) & (token >= 0) & (token < n * tokens)
+        token = dels[0, v] + row_offset
+        valid = (step < dels[1, v] - dels[0, v]) & (token >= 0) & (token < n * tokens)
         ka[:per, HD:] = jnp.where(valid, 0.0, BIG).astype(bf)
         for i in range(2):
             rows = slice(i * share, (i + 1) * share)
@@ -516,8 +532,8 @@
         ((n, width, DIL), bf),
         ((n, share * 3 // 2, 128), bf),
         ((n, width, 2 * C), bf),
-        ((n, share * 3 // 2, 128), bf),
-        ((n - 1, share * 3 // 2, 128), bf),
+        ((n, width, 2 * DEL), bf),
+        ((n - 1, width, 2 * DEL), bf),
         ((n * width, 256), bf),
         ((n, DIL * 5 // 2, 128), bf),
         ((n, DIL * 5 // 2, 128), bf),
@@ -547,7 +563,7 @@
         compiler_params=pltpu.CompilerParams(
             collective_id=0, has_side_effects=True, vmem_limit_bytes=56 * 2**20
         ),
-    )(deletions, sequence.T, conv_taps, conv_bias.reshape(1, width), w_proj.T, w_out, w_pair)
+    )(deletions.T, sequence.T, conv_taps, conv_bias.reshape(1, width), w_proj.T, w_out, w_pair)
 
 
 def local(sequence, deletions, conv_taps, conv_bias, w_proj, w_out, w_pair, dist_table):

time: 108 us -> 109 us (level)
  Pallas kernels: 104 us -> 109 us
  local copies, waits for them, and re-layouts: 3.83 us -> 0 us
    pallas_call x1, Pallas kernels: 93.9 us -> 98 us  [features(): pl.pallas_call(features_kernel, out_shape=(jax.ShapeDtypeStruct((n, part,...]
    unnamed x7 -> x0, local copies, waits for them, and re-layouts: 3.83 us -> none
where the time goes in v5:
time: 109 us
  Pallas kernels  109 us (100%)
    pallas_call x1, Pallas kernels, features(): pl.pallas_call(features_kernel, out_shape=(jax.ShapeDtypeStruct((n, part,...  98 us
    pallas_call x1, Pallas kernels, pair_map(): pl.pallas_call(functools.partial(pair_kernel, per), grid=(rows // per,),...  11.1 us

profile of v5, /device:TPU:1, one launch (start us, length us, event | category | flops | bytes accessed | tf_op | source)
XLA Modules:
  0.0 109.1 jit_solution(6587064539837639214)
XLA Ops:
  0.0 98.0 %shard_map.82 = (bf16[8,64,128]{2,1,0:T(8,128)(2,1)}, bf16[8,64,128]{2,1,0:T(8,128)(2,1)}) custom-call(s32[2,4]{1,0:T(2,128)} %bitcast.10, bf16[192,512]{1,0:T(8,128)(2,1)} %bitcast.7, f32[3,192]{1,0:T(4,128)} %taps.1, f32[1,192]{1,0:T(1,128)} %bitcast.11, bf16[448,1536]{1,0:T(8,128)(2,1)} %bitcast.6, bf16[192,1536]{1,0:T(8,128)(2,1)} %wo_ref.1, ...), custom_call_target="tpu_custom_call" | custom-call | tf_op jit(solution)/shard_map/pallas_call | solution.py:556
  98.0 11.1 %shard_map.83 = bf16[4,128,128,128]{3,2,1,0:T(8,128)(2,1)} custom-call(bf16[4,128,128]{2,1,0:T(8,128)(2,1)} %bitcast.8, bf16[4,128,128]{2,1,0:T(8,128)(2,1)} %bitcast.9, f32[16,128]{1,0:T(8,128)} %table_ref.1), custom_call_target="tpu_custom_call" | custom-call | tf_op jit(solution)/shard_map/pallas_call | solution.py:62

commit v6 on v5

--- a/solution.py
+++ b/solution.py
@@ -258,7 +258,7 @@
     ring_b0, ring_b1, ring_m, ring_p = (head_ring(buf, 10 + 9 * i) for i, buf in enumerate((gb0, gb1, gm, wp)))
     cross = {"ctx": xp, "var": 1 - g}
     ring_k0, ring_k1 = token_ring(kv0, 46, cross), token_ring(kv1, 55, cross)
-    ring_q, ring_o = token_ring(mq, 64, {"ctx": xp}), token_ring(mkv, 73, {"ctx": xp})
+    ring_o = token_ring(mkv, 73, {"ctx": xp})
 
     at = lax.broadcasted_iota(jnp.int32, (1, DIL), 1) + c * tokens
     wide = lambda k: jnp.concatenate([cols[k], cols[k]], axis=1)
@@ -280,6 +280,7 @@
         return (here + jax.nn.gelu(conv, approximate=True)).astype(bf)
 
     ring_p.begin()
+    ring_p.relay()
     halo_low.wait()
     gb0[h] = trunk(0, 0, 0)
     ring_b0.begin()
@@ -299,14 +300,10 @@
         kv[c, :count] = x[:count, HD : 2 * HD].astype(bf)
         kv[c, count:] = pack(x[:count, 2 * HD :].astype(bf))
 
+    ring_p.end()
     ring_b0.relay()
-    ring_p.relay()
+    ring_b1.relay()
     ring_b0.end()
-    x = project(gb0[...].reshape(n * width, DIL))
-    place(kv0, x, DIL)
-    ring_k0.begin()
-    queries[:DIL] = (x[:, :HD] * QSCALE).astype(bf)
-    ring_b1.relay()
 
     total = moved[c].astype(jnp.float32)
     for made in shared:
@@ -324,13 +321,15 @@
     gm[h, :width] = jnp.concatenate(made_rows[:2], axis=1)
     gm[h, width:] = jnp.concatenate([tail[: width // 2], tail[width // 2 :]], axis=1)
     ring_m.begin()
+    x = project(gb0[...].reshape(n * width, DIL))
+    place(kv0, x, DIL)
+    ring_k0.begin()
+    queries[:DIL] = (x[:, :HD] * QSCALE).astype(bf)
     ring_b1.end()
+    ring_m.relay()
     x = project(gb1[...].reshape(n * width, DIL))
     place(kv1, x, DIL)
-    ring_k1.begin()
     queries[DIL:] = (x[:, :HD] * QSCALE).astype(bf)
-    ring_m.relay()
-    ring_p.end()
     ring_m.end()
     zero = jnp.zeros((1, 128), bf)
     for k in range(n):
@@ -338,7 +337,12 @@
         flat[k * width : (k + 1) * width, 128:] = unpack_tail(gm[k, width:], zero)
     x = project(flat[...])
     mq[c] = (x[:share, :HD] * QSCALE).astype(bf)
-    ring_q.begin()
+    asked = []
+    for k in (4, 3, 5, 2, 6, 1, 7):
+        made = make(mq.at[c], mq.at[c], 64 + k, {"ctx": lax.rem(c + k, n)})
+        made.start()
+        asked.append(made)
+    ring_k1.begin()
     place(mkv, x, share)
     ring_o.begin()
     ring_k0.cross()
@@ -353,17 +357,16 @@
         return 0
 
     lax.fori_loop(0, variants, variant, 0)
-    ring_k1.cross()
-    ring_k1.relay()
-    ring_q.cross()
-    ring_q.relay()
     total = jnp.zeros((wo_ref.shape[0], 2 * C), jnp.float32)
     for k in range(0, n, 2):
         two = jnp.concatenate([wp[k], wp[k + 1]], axis=0)
         total = total + jnp.dot(wo_ref[:, k * width : (k + 2) * width], two, preferred_element_type=jnp.float32)
     mix[...] = total.astype(bf)
-    ring_q.far_block()
-    ring_q.end()
+    ring_k1.cross()
+    ring_k1.relay()
+    for k in range(1, n):
+        source = lax.rem(c + n - k, n)
+        make(mq.at[source], mq.at[source], 64 + k, {"ctx": lax.rem(c + k, n)}).wait_recv()
 
     lane = lax.broadcasted_iota(jnp.int32, (1, 128), 1)
     first = jnp.zeros((1, 128), jnp.int32)
@@ -490,9 +493,9 @@
 
     for k in range(1, n):
         make(feats.at[0], rows_buf.at[h], 90 + k, {"head": lax.rem(h + k, n)}).start()
-    for ring in (ring_b0, ring_b1, ring_m, ring_p, ring_k0, ring_k1, ring_q, ring_o):
+    for ring in (ring_b0, ring_b1, ring_m, ring_p, ring_k0, ring_k1, ring_o):
         ring.drain()
-    for made in shared:
+    for made in shared + asked:
         made.wait_send()
     for k, made in enumerate(first_sent):
         @pl.when(h != k)

time: 109 us -> 98.5 us (0.904)
  Pallas kernels: 109 us -> 98.2 us
    pallas_call x1, Pallas kernels: 98 us -> 87.1 us  [features(): pl.pallas_call(features_kernel, out_shape=(jax.ShapeDtypeStruct((n, part,...]
where the time goes in v6:
time: 98.5 us; the launch traced here: 98.3 us
  Pallas kernels  98.2 us (100%)
    pallas_call x1, Pallas kernels, features(): pl.pallas_call(features_kernel, out_shape=(jax.ShapeDtypeStruct((n, part,...  87.1 us
    pallas_call x1, Pallas kernels, pair_map(): pl.pallas_call(functools.partial(pair_kernel, per), grid=(rows // per,),...  11.1 us

profile of v6, /device:TPU:1, one launch (start us, length us, event | category | flops | bytes accessed | tf_op | source)
XLA Modules:
  0.0 98.3 jit_solution(10530998515949208970)
XLA Ops:
  0.0 87.1 %shard_map.82 = (bf16[8,64,128]{2,1,0:T(8,128)(2,1)}, bf16[8,64,128]{2,1,0:T(8,128)(2,1)}) custom-call(s32[2,4]{1,0:T(2,128)} %bitcast.10, bf16[192,512]{1,0:T(8,128)(2,1)} %bitcast.7, f32[3,192]{1,0:T(4,128)} %taps.1, f32[1,192]{1,0:T(1,128)} %bitcast.11, bf16[448,1536]{1,0:T(8,128)(2,1)} %bitcast.6, bf16[192,1536]{1,0:T(8,128)(2,1)} %wo_ref.1, ...), custom_call_target="tpu_custom_call" | custom-call | tf_op jit(solution)/shard_map/pallas_call | solution.py:559
  87.2 11.1 %shard_map.83 = bf16[4,128,128,128]{3,2,1,0:T(8,128)(2,1)} custom-call(bf16[4,128,128]{2,1,0:T(8,128)(2,1)} %bitcast.8, bf16[4,128,128]{2,1,0:T(8,128)(2,1)} %bitcast.9, f32[16,128]{1,0:T(8,128)} %table_ref.1), custom_call_target="tpu_custom_call" | custom-call | tf_op jit(solution)/shard_map/pallas_call | solution.py:62

commit v7 on v6

--- a/solution.py
+++ b/solution.py
@@ -28,30 +28,40 @@
     return hit
 
 
-def pair_kernel(rows_per, row_ref, col_ref, table_ref, out_ref, rel, rows, cols):
-    step = pl.program_id(0)
+def pair_kernel(per, row_ref, col_ref, table_ref, out_ref, rel, rows, cols, made, sem):
     span = col_ref.shape[1]
     row_count = row_ref.shape[1]
-
-    @pl.when(step == 0)
-    def _():
-        base = lax.axis_index("head") * span - lax.axis_index("ctx") * row_count - (row_count - 1)
-        dist = jnp.abs(lax.broadcasted_iota(jnp.int32, rel.shape, 0) + base)
-        value = jnp.broadcast_to(table_ref[0:1, :], rel.shape)
-        for k in range(NB - 1):
-            value = jnp.where(dist >= 2**k, table_ref[k + 1 : k + 2, :], value)
-        rel[...] = value
-        rows[...] = row_ref[...].astype(jnp.float32)
-        cols[...] = col_ref[...].astype(jnp.float32)
-
-    def one(i, _):
-        row = step * rows_per + i
-        shifted = rel[pl.ds(row_count - 1 - row, span), :]
-        for v in range(row_ref.shape[0]):
-            out_ref[v, i] = (rows[v, pl.ds(row, 1), :] + (cols[v] + shifted)).astype(out_ref.dtype)
+    base = lax.axis_index("head") * span - lax.axis_index("ctx") * row_count - (row_count - 1)
+    dist = jnp.abs(lax.broadcasted_iota(jnp.int32, rel.shape, 0) + base)
+    value = jnp.broadcast_to(table_ref[0:1, :], rel.shape)
+    for k in range(NB - 1):
+        value = jnp.where(dist >= 2**k, table_ref[k + 1 : k + 2, :], value)
+    rel[...] = value
+    rows[...] = row_ref[...].astype(jnp.float32)
+    cols[...] = col_ref[...].astype(jnp.float32)
+
+    def copy(group):
+        at = pl.ds(pl.multiple_of(group * per, per), per)
+        return pltpu.make_async_copy(made.at[:, at], out_ref.at[:, at], sem.at[group])
+
+    def one_group(group, _):
+        def one(i, _):
+            row = group * per + i
+            shifted = rel[pl.ds(row_count - 1 - row, span), :]
+            for v in range(row_ref.shape[0]):
+                made[v, row] = (rows[v, pl.ds(row, 1), :] + (cols[v] + shifted)).astype(made.dtype)
+            return 0
+
+        lax.fori_loop(0, per, one, 0, unroll=4)
+        copy(group).start()
         return 0
 
-    lax.fori_loop(0, rows_per, one, 0)
+    def done(group, _):
+        copy(group).wait()
+        return 0
+
+    lax.fori_loop(0, row_count // per, one_group, 0)
+    lax.fori_loop(0, row_count // per, done, 0)
 
 
 def pair_map(row_feats, col_feats, table):
@@ -59,16 +69,18 @@
     cols = col_feats.shape[1]
     per = 8
     vm = pl.BlockSpec(memory_space=pltpu.VMEM)
+    shape = (variants, rows, cols, C)
     return pl.pallas_call(
         functools.partial(pair_kernel, per),
-        grid=(rows // per,),
-        out_shape=jax.ShapeDtypeStruct((variants, rows, cols, C), jnp.bfloat16),
+        out_shape=jax.ShapeDtypeStruct(shape, jnp.bfloat16),
         in_specs=[vm, vm, vm],
-        out_specs=pl.BlockSpec((variants, per, cols, C), lambda i: (0, i, 0, 0)),
+        out_specs=pl.BlockSpec(memory_space=pl.ANY),
         scratch_shapes=[
             pltpu.VMEM((rows + cols, C), jnp.float32),
             pltpu.VMEM((variants, rows, C), jnp.float32),
             pltpu.VMEM((variants, cols, C), jnp.float32),
+            pltpu.VMEM(shape, jnp.bfloat16),
+            pltpu.SemaphoreType.DMA((rows // per,)),
         ],
         compiler_params=pltpu.CompilerParams(vmem_limit_bytes=60 * 2**20),
     )(row_feats, col_feats, table)
@@ -304,6 +316,15 @@
     ring_b0.relay()
     ring_b1.relay()
     ring_b0.end()
+    x = project(gb0[...].reshape(n * width, DIL))
+    place(kv0, x, DIL)
+    ring_k0.begin()
+    queries[:DIL] = (x[:, :HD] * QSCALE).astype(bf)
+    ring_b1.end()
+    x = project(gb1[...].reshape(n * width, DIL))
+    place(kv1, x, DIL)
+    ring_k1.begin()
+    queries[DIL:] = (x[:, :HD] * QSCALE).astype(bf)
 
     total = moved[c].astype(jnp.float32)
     for made in shared:
@@ -321,15 +342,9 @@
     gm[h, :width] = jnp.concatenate(made_rows[:2], axis=1)
     gm[h, width:] = jnp.concatenate([tail[: width // 2], tail[width // 2 :]], axis=1)
     ring_m.begin()
-    x = project(gb0[...].reshape(n * width, DIL))
-    place(kv0, x, DIL)
-    ring_k0.begin()
-    queries[:DIL] = (x[:, :HD] * QSCALE).astype(bf)
-    ring_b1.end()
+    ring_k0.cross()
+    ring_k0.relay()
     ring_m.relay()
-    x = project(gb1[...].reshape(n * width, DIL))
-    place(kv1, x, DIL)
-    queries[DIL:] = (x[:, :HD] * QSCALE).astype(bf)
     ring_m.end()
     zero = jnp.zeros((1, 128), bf)
     for k in range(n):
@@ -342,11 +357,10 @@
         made = make(mq.at[c], mq.at[c], 64 + k, {"ctx": lax.rem(c + k, n)})
         made.start()
         asked.append(made)
-    ring_k1.begin()
     place(mkv, x, share)
     ring_o.begin()
-    ring_k0.cross()
-    ring_k0.relay()
+    ring_k1.cross()
+    ring_k1.relay()
 
     def variant(v, _):
         first = dels[0, v]
@@ -362,8 +376,7 @@
         two = jnp.concatenate([wp[k], wp[k + 1]], axis=0)
         total = total + jnp.dot(wo_ref[:, k * width : (k + 2) * width], two, preferred_element_type=jnp.float32)
     mix[...] = total.astype(bf)
-    ring_k1.cross()
-    ring_k1.relay()
+    ring_k0.far_block()
     for k in range(1, n):
         source = lax.rem(c + n - k, n)
         make(mq.at[source], mq.at[source], 64 + k, {"ctx": lax.rem(c + k, n)}).wait_recv()
@@ -424,7 +437,6 @@
         return 0
 
     lax.fori_loop(0, 2, attend, 0)
-    ring_k0.far_block()
     ring_k1.far_block()
     ring_o.cross()
     ring_o.relay()

time: 98.5 us -> 90.5 us (0.919)
  Pallas kernels: 98.2 us -> 90.1 us
    pallas_call x1, Pallas kernels: 87.1 us -> 82.9 us  [features(): pl.pallas_call(features_kernel, out_shape=(jax.ShapeDtypeStruct((n, part,...]
    pallas_call x1, Pallas kernels: 11.1 us -> 7.29 us  [pair_map(): pl.pallas_call(functools.partial(pair_kernel, per), out_shape=jax.ShapeDt...]
where the time goes in v7:
time: 90.5 us; the launch traced here: 90.3 us
  Pallas kernels  90.1 us (100%)
    pallas_call x1, Pallas kernels, features(): pl.pallas_call(features_kernel, out_shape=(jax.ShapeDtypeStruct((n, part,...  82.9 us
    pallas_call x1, Pallas kernels, pair_map(): pl.pallas_call(functools.partial(pair_kernel, per), out_shape=jax.ShapeDt...  7.29 us

profile of v7, /device:TPU:1, one launch (start us, length us, event | category | flops | bytes accessed | tf_op | source)
XLA Modules:
  0.0 90.3 jit_solution(12891944268790993351)
XLA Ops:
  0.0 82.9 %shard_map.82 = (bf16[8,64,128]{2,1,0:T(8,128)(2,1)}, bf16[8,64,128]{2,1,0:T(8,128)(2,1)}) custom-call(s32[2,4]{1,0:T(2,128)} %bitcast.10, bf16[192,512]{1,0:T(8,128)(2,1)} %bitcast.7, f32[3,192]{1,0:T(4,128)} %taps.1, f32[1,192]{1,0:T(1,128)} %bitcast.11, bf16[448,1536]{1,0:T(8,128)(2,1)} %bitcast.6, bf16[192,1536]{1,0:T(8,128)(2,1)} %wo_ref.1, ...), custom_call_target="tpu_custom_call" | custom-call | tf_op jit(solution)/shard_map/pallas_call | solution.py:571
  82.9 7.3 %shard_map.83 = bf16[4,128,128,128]{3,2,1,0:T(8,128)(2,1)} custom-call(bf16[4,128,128]{2,1,0:T(8,128)(2,1)} %bitcast.8, bf16[4,128,128]{2,1,0:T(8,128)(2,1)} %bitcast.9, f32[16,128]{1,0:T(8,128)} %table_ref.1), custom_call_target="tpu_custom_call" | custom-call | tf_op jit(solution)/shard_map/pallas_call | solution.py:73

commit v8 on v7

--- a/solution.py
+++ b/solution.py
@@ -148,6 +148,8 @@
 
 
 class TokenRing(Ring):
+    near_only = False
+
     def begin(self):
         self.send(self.me, self.full, 2, self.to_mate)
         self.send(self.me, self.full, 0, self.to_up)
@@ -165,14 +167,25 @@
         self.send(self.up, self.hi, 5, self.to_dn)
 
     def far_block(self):
+        if self.near_only:
+            dn, up = self.mate_of(self.dn), self.mate_of(self.up)
+            self.got(dn, self.full, 4)
+            self.send(dn, self.lo, 7, self.to_up)
+            self.got(up, self.full, 6)
+            self.send(up, self.hi, 8, self.to_dn)
+            return
         self.got(self.far, self.lo, 3)
         self.send(self.far, self.lo, 7, self.to_mate)
         self.got(self.far, self.hi, 5)
         self.send(self.far, self.hi, 8, self.to_mate)
 
     def end(self):
-        self.got(self.mate_of(self.dn), self.full, 4)
-        self.got(self.mate_of(self.up), self.full, 6)
+        if self.near_only:
+            self.got(self.far, self.lo, 3)
+            self.got(self.far, self.hi, 5)
+        else:
+            self.got(self.mate_of(self.dn), self.full, 4)
+            self.got(self.mate_of(self.up), self.full, 6)
         self.got(self.mate_of(self.far), self.lo, 7)
         self.got(self.mate_of(self.far), self.hi, 8)
 
@@ -252,12 +265,8 @@
     halo_high = make(seq.at[:, pl.ds(0, DIL)], high, 1, {"ctx": lax.rem(c + 7, n)})
     halo_low.start()
     halo_high.start()
-    shared = []
-    for k in (4, 3, 5, 2, 6, 1, 7):
-        to = lax.rem(c + k, n)
-        made = make(moved.at[to], landed.at[k - 1], 1 + k, {"ctx": to})
-        made.start()
-        shared.append(made)
+    shared = [make(moved.at[pl.ds(4 - x0, 4)], landed.at[pl.ds(0, 4)], 2, {"ctx": xp})]
+    shared[0].start()
 
     def head_ring(buf, base):
         return HeadRing(make, buf, buf.shape[1], base, h, dn_h, up_h, far_h, sib, sib_of,
@@ -271,6 +280,7 @@
     cross = {"ctx": xp, "var": 1 - g}
     ring_k0, ring_k1 = token_ring(kv0, 46, cross), token_ring(kv1, 55, cross)
     ring_o = token_ring(mkv, 73, {"ctx": xp})
+    ring_o.near_only = True
 
     at = lax.broadcasted_iota(jnp.int32, (1, DIL), 1) + c * tokens
     wide = lambda k: jnp.concatenate([cols[k], cols[k]], axis=1)
@@ -319,6 +329,14 @@
     x = project(gb0[...].reshape(n * width, DIL))
     place(kv0, x, DIL)
     ring_k0.begin()
+    shared[0].wait_recv()
+    for k in range(4):
+        moved[x0 + k] = moved[x0 + k] + landed[k]
+    for k in (2, 1, 3):
+        to = x0 + lax.rem(y0 + k, 4)
+        made = make(moved.at[to], landed.at[3 + k], 2 + k, {"ctx": to})
+        made.start()
+        shared.append(made)
     queries[:DIL] = (x[:, :HD] * QSCALE).astype(bf)
     ring_b1.end()
     x = project(gb1[...].reshape(n * width, DIL))
@@ -327,10 +345,10 @@
     queries[DIL:] = (x[:, :HD] * QSCALE).astype(bf)
 
     total = moved[c].astype(jnp.float32)
-    for made in shared:
+    for made in shared[1:]:
         made.wait_recv()
-    for k in range(1, n):
-        total = total + landed[k - 1].astype(jnp.float32)
+    for k in range(4, 7):
+        total = total + landed[k].astype(jnp.float32)
     runs = [total[:, i * run : (i + 1) * run] for i in range(4)]
     nil = jnp.zeros((width, run), jnp.float32)
     t0, t1, t2, t3 = (cols[k, :, :run] for k in range(4))
@@ -353,14 +371,22 @@
     x = project(flat[...])
     mq[c] = (x[:share, :HD] * QSCALE).astype(bf)
     asked = []
-    for k in (4, 3, 5, 2, 6, 1, 7):
-        made = make(mq.at[c], mq.at[c], 64 + k, {"ctx": lax.rem(c + k, n)})
-        made.start()
-        asked.append(made)
+
+    def hand_on(slot, index):
+        for k in (2, 1, 3):
+            made = make(mq.at[slot], mq.at[slot], index + k, {"ctx": x0 + lax.rem(y0 + k, 4)})
+            made.start()
+            asked.append(made)
+
+    asked.append(make(mq.at[c], mq.at[c], 64, {"ctx": xp}))
+    asked[0].start()
+    hand_on(c, 64)
     place(mkv, x, share)
-    ring_o.begin()
     ring_k1.cross()
     ring_k1.relay()
+    make(mq.at[xp], mq.at[xp], 64, {"ctx": xp}).wait_recv()
+    hand_on(xp, 67)
+    ring_o.begin()
 
     def variant(v, _):
         first = dels[0, v]
@@ -377,9 +403,10 @@
         total = total + jnp.dot(wo_ref[:, k * width : (k + 2) * width], two, preferred_element_type=jnp.float32)
     mix[...] = total.astype(bf)
     ring_k0.far_block()
-    for k in range(1, n):
-        source = lax.rem(c + n - k, n)
-        make(mq.at[source], mq.at[source], 64 + k, {"ctx": lax.rem(c + k, n)}).wait_recv()
+    for k in range(1, 4):
+        near = x0 + lax.rem(y0 + 4 - k, 4)
+        for source, index in ((near, 64), (other(near), 67)):
+            make(mq.at[source], mq.at[source], index + k, {"ctx": near}).wait_recv()
 
     lane = lax.broadcasted_iota(jnp.int32, (1, 128), 1)
     first = jnp.zeros((1, 128), jnp.int32)

time: 90.5 us -> 98.8 us (1.092)
  Pallas kernels: 90.1 us -> 98.3 us
    pallas_call x1, Pallas kernels: 82.9 us -> 91.1 us  [features(): pl.pallas_call(features_kernel, out_shape=(jax.ShapeDtypeStruct((n, part,...]
where the time goes in v8:
time: 98.8 us; the launch traced here: 98.5 us
  Pallas kernels  98.3 us (99%)
    pallas_call x1, Pallas kernels, features(): pl.pallas_call(features_kernel, out_shape=(jax.ShapeDtypeStruct((n, part,...  91.1 us
    pallas_call x1, Pallas kernels, pair_map(): pl.pallas_call(functools.partial(pair_kernel, per), out_shape=jax.ShapeDt...  7.29 us

profile of v8, /device:TPU:1, one launch (start us, length us, event | category | flops | bytes accessed | tf_op | source)
XLA Modules:
  0.0 98.5 jit_solution(2151370409222627429)
XLA Ops:
  0.0 91.1 %shard_map.82 = (bf16[8,64,128]{2,1,0:T(8,128)(2,1)}, bf16[8,64,128]{2,1,0:T(8,128)(2,1)}) custom-call(s32[2,4]{1,0:T(2,128)} %bitcast.10, bf16[192,512]{1,0:T(8,128)(2,1)} %bitcast.7, f32[3,192]{1,0:T(4,128)} %taps.1, f32[1,192]{1,0:T(1,128)} %bitcast.11, bf16[448,1536]{1,0:T(8,128)(2,1)} %bitcast.6, bf16[192,1536]{1,0:T(8,128)(2,1)} %wo_ref.1, ...), custom_call_target="tpu_custom_call" | custom-call | tf_op jit(solution)/shard_map/pallas_call | solution.py:598
  91.1 7.3 %shard_map.83 = bf16[4,128,128,128]{3,2,1,0:T(8,128)(2,1)} custom-call(bf16[4,128,128]{2,1,0:T(8,128)(2,1)} %bitcast.8, bf16[4,128,128]{2,1,0:T(8,128)(2,1)} %bitcast.9, f32[16,128]{1,0:T(8,128)} %table_ref.1), custom_call_target="tpu_custom_call" | custom-call | tf_op jit(solution)/shard_map/pallas_call | solution.py:73

commit v9 on v7

--- a/solution.py
+++ b/solution.py
@@ -191,10 +191,10 @@
     return jnp.where(keep, both, jnp.broadcast_to(fill, both.shape))
 
 
-def features_kernel(dels, seq, taps, bias, w_ref, wo_ref, wp_ref, row_out, col_out,
+def features_kernel(dels, seq, taps, bias, w_hbm, wo_hbm, wp_ref, row_out, col_out,
                     low, high, cols, gb0, gb1, gm, wp, moved, landed, flat, kv0, kv1, mq, mkv,
-                    queries, q_aug, top, acc, ka, va, pooled, mix, mine, arrived, rows_buf, cols_buf, feats,
-                    send, recv):
+                    queries, q_aug, top, acc, ka, va, pooled, mix, mine, arrived, rows_buf, cols_buf, feats, w_ref, wo_ref,
+                    send, recv, fetched):
     width, tokens = seq.shape
     variants = dels.shape[1]
     share = SEGS * DEL // 2
@@ -210,6 +210,12 @@
     xp = other(c)
     sib_of = lambda t: t + 1 - 2 * lax.rem(t, 2)
 
+    fetch = [
+        pltpu.make_async_copy(w_hbm, w_ref, fetched.at[0]),
+        pltpu.make_async_copy(wo_hbm, wo_ref, fetched.at[1]),
+    ]
+    for made in fetch:
+        made.start()
     barrier = pltpu.get_barrier_semaphore()
     peers = [{"ctx": lax.rem(c + k, n)} for k in range(1, n)]
     peers += [{"head": lax.rem(h + k, n)} for k in range(1, n)]
@@ -315,6 +321,8 @@
     ring_p.end()
     ring_b0.relay()
     ring_b1.relay()
+    for made in fetch:
+        made.wait()
     ring_b0.end()
     x = project(gb0[...].reshape(n * width, DIL))
     place(kv0, x, DIL)
@@ -436,15 +444,19 @@
             unit(v, ka[...], va[...])
         return 0
 
-    lax.fori_loop(0, 2, attend, 0)
-    ring_k1.far_block()
+    lax.fori_loop(0, 1, attend, 0)
     ring_o.cross()
     ring_o.relay()
-    lax.fori_loop(2, 5, attend, 0)
+    ring_k1.far_block()
+    lax.fori_loop(1, 4, attend, 0)
+    ring_o.far_block()
     ring_k0.end()
     ring_k1.end()
-    ring_o.far_block()
-    lax.fori_loop(5, n, attend, 0)
+    lax.fori_loop(4, n, attend, 0)
+    for ring in (ring_b0, ring_b1, ring_m, ring_p, ring_k0, ring_k1):
+        ring.drain()
+    for made in shared + asked:
+        made.wait_send()
     ring_o.end()
 
     row = lax.broadcasted_iota(jnp.int32, (per, 128), 0)
@@ -505,10 +517,7 @@
 
     for k in range(1, n):
         make(feats.at[0], rows_buf.at[h], 90 + k, {"head": lax.rem(h + k, n)}).start()
-    for ring in (ring_b0, ring_b1, ring_m, ring_p, ring_k0, ring_k1, ring_o):
-        ring.drain()
-    for made in shared + asked:
-        made.wait_send()
+    ring_o.drain()
     for k, made in enumerate(first_sent):
         @pl.when(h != k)
         def _():
@@ -567,14 +576,16 @@
         ((n, part, C), bf),
         ((n, part, C), bf),
         ((2, part, C), bf),
+        ((w_proj.shape[1], w_proj.shape[0]), bf),
+        (w_out.shape, bf),
     ]
     return pl.pallas_call(
         features_kernel,
         out_shape=(jax.ShapeDtypeStruct((n, part, C), bf),) * 2,
-        in_specs=[pl.BlockSpec(memory_space=pltpu.SMEM)] + [vm] * 6,
+        in_specs=[pl.BlockSpec(memory_space=pltpu.SMEM)] + [vm] * 3 + [pl.BlockSpec(memory_space=pl.ANY)] * 2 + [vm],
         out_specs=(vm, vm),
         scratch_shapes=[pltpu.VMEM(shape, kind) for shape, kind in scratch]
-        + [pltpu.SemaphoreType.DMA((106,)), pltpu.SemaphoreType.DMA((106,))],
+        + [pltpu.SemaphoreType.DMA((106,)), pltpu.SemaphoreType.DMA((106,)), pltpu.SemaphoreType.DMA((2,))],
         compiler_params=pltpu.CompilerParams(
             collective_id=0, has_side_effects=True, vmem_limit_bytes=56 * 2**20
         ),

time: 90.5 us -> 92.6 us (1.023)
  Pallas kernels: 90.1 us -> 92.1 us
    pallas_call x1, Pallas kernels: 82.9 us -> 84.8 us  [features(): pl.pallas_call(features_kernel, out_shape=(jax.ShapeDtypeStruct((n, part,...]
where the time goes in v9:
time: 92.6 us; the launch traced here: 92.2 us
  Pallas kernels  92.1 us (99%)
    pallas_call x1, Pallas kernels, features(): pl.pallas_call(features_kernel, out_shape=(jax.ShapeDtypeStruct((n, part,...  84.8 us
    pallas_call x1, Pallas kernels, pair_map(): pl.pallas_call(functools.partial(pair_kernel, per), out_shape=jax.ShapeDt...  7.29 us

profile of v9, /device:TPU:1, one launch (start us, length us, event | category | flops | bytes accessed | tf_op | source)
XLA Modules:
  0.0 92.2 jit_solution(1701094529378333833)
XLA Ops:
  0.0 84.8 %shard_map.82 = (bf16[8,64,128]{2,1,0:T(8,128)(2,1)}, bf16[8,64,128]{2,1,0:T(8,128)(2,1)}) custom-call(s32[2,4]{1,0:T(2,128)} %bitcast.10, bf16[192,512]{1,0:T(8,128)(2,1)} %bitcast.7, f32[3,192]{1,0:T(4,128)} %taps.1, f32[1,192]{1,0:T(1,128)} %bitcast.11, bf16[448,1536]{1,0:T(8,128)(2,1)} %bitcast.6, bf16[192,1536]{1,0:T(8,128)(2,1)} %wo_hbm.1, ...), custom_call_target="tpu_custom_call" | custom-call | tf_op jit(solution)/shard_map/pallas_call | solution.py:582
  84.8 7.3 %shard_map.83 = bf16[4,128,128,128]{3,2,1,0:T(8,128)(2,1)} custom-call(bf16[4,128,128]{2,1,0:T(8,128)(2,1)} %bitcast.8, bf16[4,128,128]{2,1,0:T(8,128)(2,1)} %bitcast.9, f32[16,128]{1,0:T(8,128)} %table_ref.1), custom_call_target="tpu_custom_call" | custom-call | tf_op jit(solution)/shard_map/pallas_call | solution.py:73

commit v10 on v9

--- a/solution.py
+++ b/solution.py
@@ -444,19 +444,15 @@
             unit(v, ka[...], va[...])
         return 0
 
-    lax.fori_loop(0, 1, attend, 0)
+    lax.fori_loop(0, 2, attend, 0)
+    ring_k1.far_block()
     ring_o.cross()
     ring_o.relay()
-    ring_k1.far_block()
-    lax.fori_loop(1, 4, attend, 0)
-    ring_o.far_block()
+    lax.fori_loop(2, 5, attend, 0)
     ring_k0.end()
     ring_k1.end()
-    lax.fori_loop(4, n, attend, 0)
-    for ring in (ring_b0, ring_b1, ring_m, ring_p, ring_k0, ring_k1):
-        ring.drain()
-    for made in shared + asked:
-        made.wait_send()
+    ring_o.far_block()
+    lax.fori_loop(5, n, attend, 0)
     ring_o.end()
 
     row = lax.broadcasted_iota(jnp.int32, (per, 128), 0)
@@ -517,7 +513,10 @@
 
     for k in range(1, n):
         make(feats.at[0], rows_buf.at[h], 90 + k, {"head": lax.rem(h + k, n)}).start()
-    ring_o.drain()
+    for ring in (ring_b0, ring_b1, ring_m, ring_p, ring_k0, ring_k1, ring_o):
+        ring.drain()
+    for made in shared + asked:
+        made.wait_send()
     for k, made in enumerate(first_sent):
         @pl.when(h != k)
         def _():

time: 92.6 us -> 89.9 us (0.971)
  Pallas kernels: 92.1 us -> 89.6 us
    pallas_call x1, Pallas kernels: 84.8 us -> 82.3 us  [features(): pl.pallas_call(features_kernel, out_shape=(jax.ShapeDtypeStruct((n, part,...]
where the time goes in v10:
time: 89.9 us; the launch traced here: 89.8 us
  Pallas kernels  89.6 us (100%)
    pallas_call x1, Pallas kernels, features(): pl.pallas_call(features_kernel, out_shape=(jax.ShapeDtypeStruct((n, part,...  82.3 us
    pallas_call x1, Pallas kernels, pair_map(): pl.pallas_call(functools.partial(pair_kernel, per), out_shape=jax.ShapeDt...  7.29 us

profile of v10, /device:TPU:1, one launch (start us, length us, event | category | flops | bytes accessed | tf_op | source)
XLA Modules:
  0.0 89.8 jit_solution(10757772587954055089)
XLA Ops:
  0.0 82.3 %shard_map.82 = (bf16[8,64,128]{2,1,0:T(8,128)(2,1)}, bf16[8,64,128]{2,1,0:T(8,128)(2,1)}) custom-call(s32[2,4]{1,0:T(2,128)} %bitcast.10, bf16[192,512]{1,0:T(8,128)(2,1)} %bitcast.7, f32[3,192]{1,0:T(4,128)} %taps.1, f32[1,192]{1,0:T(1,128)} %bitcast.11, bf16[448,1536]{1,0:T(8,128)(2,1)} %bitcast.6, bf16[192,1536]{1,0:T(8,128)(2,1)} %wo_hbm.1, ...), custom_call_target="tpu_custom_call" | custom-call | tf_op jit(solution)/shard_map/pallas_call | solution.py:581
  82.3 7.3 %shard_map.83 = bf16[4,128,128,128]{3,2,1,0:T(8,128)(2,1)} custom-call(bf16[4,128,128]{2,1,0:T(8,128)(2,1)} %bitcast.8, bf16[4,128,128]{2,1,0:T(8,128)(2,1)} %bitcast.9, f32[16,128]{1,0:T(8,128)} %table_ref.1), custom_call_target="tpu_custom_call" | custom-call | tf_op jit(solution)/shard_map/pallas_call | solution.py:73

commit v11 on v10

--- a/solution.py
+++ b/solution.py
@@ -453,6 +453,10 @@
     ring_k1.end()
     ring_o.far_block()
     lax.fori_loop(5, n, attend, 0)
+    for ring in (ring_b0, ring_b1, ring_m, ring_p, ring_k0, ring_k1):
+        ring.drain()
+    for made in shared + asked:
+        made.wait_send()
     ring_o.end()
 
     row = lax.broadcasted_iota(jnp.int32, (per, 128), 0)
@@ -513,10 +517,7 @@
 
     for k in range(1, n):
         make(feats.at[0], rows_buf.at[h], 90 + k, {"head": lax.rem(h + k, n)}).start()
-    for ring in (ring_b0, ring_b1, ring_m, ring_p, ring_k0, ring_k1, ring_o):
-        ring.drain()
-    for made in shared + asked:
-        made.wait_send()
+    ring_o.drain()
     for k, made in enumerate(first_sent):
         @pl.when(h != k)
         def _():

time: 89.9 us -> 90 us (level)
  no operation moved by 1% of the time
where the time goes in v11:
time: 90 us; the launch traced here: 89.8 us
  Pallas kernels  89.7 us (100%)
    pallas_call x1, Pallas kernels, features(): pl.pallas_call(features_kernel, out_shape=(jax.ShapeDtypeStruct((n, part,...  82.4 us
    pallas_call x1, Pallas kernels, pair_map(): pl.pallas_call(functools.partial(pair_kernel, per), out_shape=jax.ShapeDt...  7.29 us

profile of v11, /device:TPU:1, one launch (start us, length us, event | category | flops | bytes accessed | tf_op | source)
XLA Modules:
  0.0 89.8 jit_solution(1394569649500055751)
XLA Ops:
  0.0 82.4 %shard_map.82 = (bf16[8,64,128]{2,1,0:T(8,128)(2,1)}, bf16[8,64,128]{2,1,0:T(8,128)(2,1)}) custom-call(s32[2,4]{1,0:T(2,128)} %bitcast.10, bf16[192,512]{1,0:T(8,128)(2,1)} %bitcast.7, f32[3,192]{1,0:T(4,128)} %taps.1, f32[1,192]{1,0:T(1,128)} %bitcast.11, bf16[448,1536]{1,0:T(8,128)(2,1)} %bitcast.6, bf16[192,1536]{1,0:T(8,128)(2,1)} %wo_hbm.1, ...), custom_call_target="tpu_custom_call" | custom-call | tf_op jit(solution)/shard_map/pallas_call | solution.py:582
  82.4 7.3 %shard_map.83 = bf16[4,128,128,128]{3,2,1,0:T(8,128)(2,1)} custom-call(bf16[4,128,128]{2,1,0:T(8,128)(2,1)} %bitcast.8, bf16[4,128,128]{2,1,0:T(8,128)(2,1)} %bitcast.9, f32[16,128]{1,0:T(8,128)} %table_ref.1), custom_call_target="tpu_custom_call" | custom-call | tf_op jit(solution)/shard_map/pallas_call | solution.py:73
